TPU v7x, 32 devices: a whole 2x2x4 slice. The times are simulated.
32 devices in a mesh: groups: 2 (over x), rows: 16 (over z, y, core).
Axes of the slice: x: 2, y: 2, z: 4, core: 2. Of those that a mesh axis runs over, the one named last changes fastest.
Arguments:
- dictionary: bfloat16 [8192, 32768], P('rows'), may hold values from -0.0625 to 0.0625
- patches: bfloat16 [8192, 2048], P('rows', 'groups'), parts along dimension 1, may hold values from -6 to 6
- initial_codes: bfloat16 [32, 16, 4096], P(('groups', 'rows')), parts along dimension 0, may hold values from -3 to 3
- support: int32 [32, 16], P('groups'), parts along dimension 0, may hold values from 0 to 511, as said below
- counts: int32 [32], P('groups'), parts along dimension 0, may hold values from 4 to 16, as said below
- group_order: int32 [32], P('groups'), parts along dimension 0, may hold values from 0 to 15, each once
- penalty: float32 [32, 64], P('groups'), parts along dimension 0, may hold values from 0.05 to 0.5
Outputs:
- codes: float32 [32, 16, 4096], P(('groups', 'rows')), parts along dimension 0
There are 2 independent parts, one for each index of `groups`. A program takes and returns all parts, laid end to end along the dimension named above; an argument that names none is the same for every part. Nothing has to cross between parts.
Inputs may be any that keep to these rules, and one draw needn't show every extreme that they name: `support`: in each group's list the first counts entries are distinct block ids; entries at positions counts and beyond are padding and are ignored. The counts of one part sum to exactly 160.
All inputs are finite; a program needn't handle non-finite values.
Results may differ from a plain program's by a relative error of at most 0.0055.
Values may be sent and summed in bfloat16 or wider, within the bound.
No kernel may reach another device: no remote copies, remote signals or barrier semaphores. Data moves between devices by JAX's collectives and lax.ppermute only.
A program may use at most 192 MiB of HBM per device.

v0:
```python
import functools

import jax
import jax.numpy as jnp
from jax import lax
from jax.experimental import pallas as pl
from jax.experimental.pallas import tpu as pltpu
from jax.sharding import PartitionSpec as P

BLOCK = 64
SLOTS = 16
PATCHES = 64
ITERS = 3
MEAN_LIVE = 10
LANES = 2 * BLOCK
SLOT_PAIRS = SLOTS // 2
VMEM_LIMIT = 32 * 1024 * 1024
SUPPORT_VMEM = 58 * 1024 * 1024


def momentum_list():
    values = []
    tvalue = 1.0
    for turn in range(ITERS):
        tnext = (1.0 + (1.0 + 4.0 * tvalue * tvalue) ** 0.5) / 2.0
        values.append((tvalue - 1.0) / tnext)
        tvalue = tnext
    return values


def swap_halves(value):
    return jnp.concatenate([value[:, BLOCK:], value[:, :BLOCK]], axis=1)


def upper_half(shape):
    return lax.broadcasted_iota(jnp.int32, shape, 1) >= BLOCK


def support_kernel(begin, order, support, counts, dictionary, out, held, picks, ids, sems, out_sems):
    entries, rows, _ = held.shape
    pairs = entries // 2

    def fetch(entry, block):
        start = pl.multiple_of((block // 2) * LANES, LANES)
        return pltpu.make_async_copy(dictionary.at[:, pl.ds(start, LANES)], held.at[entry], sems.at[entry])

    def start_group(index, offset):
        group = order[index]
        live = counts[group]

        def start_slot(slot, carry):
            block = support[group, slot]
            ids[offset + slot] = block
            fetch(offset + slot, block).start()
            return carry

        lax.fori_loop(jnp.clip(-offset, 0, live), jnp.clip(entries - offset, 0, live), start_slot, 0)
        return offset + live

    lax.fori_loop(0, order.shape[0], start_group, jnp.int32(-begin))
    shape = (2 * LANES, LANES)
    source = lax.broadcasted_iota(jnp.int32, shape, 0)
    target = lax.broadcasted_iota(jnp.int32, shape, 1)
    for choice in range(4):
        wanted = jnp.where(target < BLOCK, (choice % 2) * BLOCK + target, LANES + (choice // 2) * BLOCK + target - BLOCK)
        picks[choice] = (source == wanted).astype(jnp.float32).astype(jnp.bfloat16)

    def store(pair):
        return pltpu.make_async_copy(held.at[2 * pair], out.at[pair], out_sems.at[pair])

    def pack(step, carry):
        for pair in (2 * step, 2 * step + 1):
            fetch(2 * pair, ids[2 * pair]).wait()
            fetch(2 * pair + 1, ids[2 * pair + 1]).wait()
        packed = []
        for pair in (2 * step, 2 * step + 1):
            choice = ids[2 * pair] % 2 + 2 * (ids[2 * pair + 1] % 2)
            both = jnp.concatenate([held[2 * pair], held[2 * pair + 1]], axis=1)
            packed.append(jnp.dot(both, picks[choice], preferred_element_type=jnp.float32).astype(jnp.bfloat16))
        for pair, value in zip((2 * step, 2 * step + 1), packed):
            held[2 * pair] = value
            store(pair).start()
        return carry

    lax.fori_loop(0, pairs // 2, pack, 0)

    def drain(pair, carry):
        store(pair).wait()
        return carry

    lax.fori_loop(0, pairs, drain, 0)


def collect_support(order, support, counts, dictionary, begin, entries):
    rows = dictionary.shape[0]
    pairs = entries // 2
    return pl.pallas_call(
        functools.partial(support_kernel, begin),
        grid_spec=pltpu.PrefetchScalarGridSpec(
            num_scalar_prefetch=3,
            grid=(),
            in_specs=[pl.BlockSpec(memory_space=pl.ANY)],
            out_specs=pl.BlockSpec(memory_space=pl.ANY),
            scratch_shapes=[
                pltpu.VMEM((entries, rows, LANES), dictionary.dtype),
                pltpu.VMEM((4, 2 * LANES, LANES), jnp.bfloat16),
                pltpu.SMEM((entries,), jnp.int32),
                pltpu.SemaphoreType.DMA((entries,)),
                pltpu.SemaphoreType.DMA((pairs,)),
            ],
        ),
        out_shape=jax.ShapeDtypeStruct((pairs, rows, LANES), dictionary.dtype),
        compiler_params=pltpu.CompilerParams(vmem_limit_bytes=SUPPORT_VMEM),
        cost_estimate=pl.CostEstimate(
            flops=0, transcendentals=0, bytes_accessed=3 * pairs * rows * LANES * 2
        ),
        name="collect_support",
    )(order, support, counts, dictionary)


def relative_slot(index, me, devices):
    apart = index ^ me
    return (apart % 2) * (devices // 2) + ((apart // 2) % 2) * (devices // 4) + apart // 4


def gradient_kernel(
    packed_in, packed_out, shards, order, counts, own, blocks, blocks_b, near, far, targets, keep, send, extra,
    held, codes, total, start_codes, offsets, sems, code_sems,
):
    groups = order.shape[0]
    me = own[0]
    pairs = 2 * blocks.shape[0]
    piece = pairs // shards
    half_in = near.shape[0]
    shard_in = 2 * half_in // shards
    half_out = keep.shape[0]
    shard_out = 2 * half_out // shards

    def load(index, source=blocks, begin=0):
        span = pl.ds(index * piece, piece)
        return pltpu.make_async_copy(source.at[pl.ds(begin, piece)], held.at[span], sems.at[index])

    code_loads = [
        pltpu.make_async_copy(near, codes.at[pl.ds(0, half_in)], code_sems.at[0]),
        pltpu.make_async_copy(far, codes.at[pl.ds(half_in, half_in)], code_sems.at[1]),
    ]
    for copy in code_loads:
        copy.start()
    for index in range(shards):
        source = (blocks, blocks_b)[2 * index // shards]
        load(index, source, (index % (shards // 2)) * piece).start()
    held[pairs:] = jnp.zeros((held.shape[0] - pairs,) + held.shape[1:], held.dtype)
    for copy in code_loads:
        copy.wait()

    upper = upper_half((PATCHES, LANES))
    side = upper.astype(jnp.int32)

    def place(pair, shard):
        holder = pair // shard
        return relative_slot(holder, me, shards) * shard + (pair - holder * shard)

    def spot_of(pair, shard):
        return jnp.where(pair < pairs, place(jnp.minimum(pair, pairs - 1), shard), pair)

    def shifted(parts, count, odd, ahead):
        turned = [swap_halves(part) for part in parts]
        last = len(parts) - 1
        moved = []
        for pair in range(count):
            low, high = (pair, pair + 1) if ahead else (pair - 1, pair)
            low, high = min(max(low, 0), last), min(max(high, 0), last)
            value = jnp.where(upper, turned[high], turned[low])
            moved.append(jnp.where(odd, value, parts[min(pair, last)]))
        return moved

    def read_codes(index, offset, live, count):
        first = offset // 2
        if packed_in:
            parts = [codes[place(jnp.minimum(first + pair, pairs - 1), shard_in)] for pair in range(count)]
        else:
            base = place(index * SLOT_PAIRS, shard_in)
            slots = min(count, SLOT_PAIRS)
            parts = shifted([codes[base + pair] for pair in range(slots)], count, offset % 2 == 1, False)
        masked = []
        for pair, part in enumerate(parts):
            entry = 2 * (first + pair) + side
            mine = (entry >= offset) & (entry < offset + live)
            masked.append(jnp.where(mine, part, jnp.zeros_like(part)))
        return masked

    def write_packed(ref, parts, offset, shard):
        first = offset // 2
        for pair, part in enumerate(parts):
            spot = spot_of(first + pair, shard)
            if pair == 0:
                part = jnp.where(upper | (offset % 2 == 0), part, ref[spot])
            ref[spot] = part

    def one_group(index, offset, live, count):
        first = offset // 2
        parts = read_codes(index, offset, live, count)
        if packed_out and not packed_in:
            first_pair = offset // 2
            for pair, part in enumerate(parts):
                if pair == 0:
                    part = jnp.where(upper | (offset % 2 == 0), part, start_codes[first_pair])
                start_codes[first_pair + pair] = part
        matrix = jnp.concatenate([held[first + pair] for pair in range(count)], axis=1)
        point = jnp.concatenate(parts, axis=1)
        residual = lax.dot_general(point, matrix, (((1,), (1,)), ((), ())), preferred_element_type=jnp.float32)
        column = pl.multiple_of(order[index] * PATCHES, PATCHES)
        target = targets[pl.ds(column, PATCHES), :].astype(jnp.float32)
        residual = (residual - target).astype(jnp.bfloat16)
        gradient = jnp.dot(residual, matrix, preferred_element_type=jnp.float32)
        grads = [gradient[:, pair * LANES : (pair + 1) * LANES] for pair in range(count)]
        if packed_out:
            write_packed(total, grads, offset, shard_out)
        else:
            base = place(index * SLOT_PAIRS, shard_out)
            moved = shifted(grads, min(count, SLOT_PAIRS), offset % 2 == 1, True)
            for pair in range(SLOT_PAIRS):
                if pair < len(moved):
                    value = jnp.where(2 * pair + side < live, moved[pair], 0.0)
                else:
                    value = jnp.zeros((PATCHES, LANES), jnp.float32)
                total[base + pair] = value

    def two_groups(step, carry):
        offset, waited = carry
        picks = []
        chunks = 1
        for index in (2 * step, 2 * step + 1):
            live = counts[order[index]]
            offsets[index] = offset
            picks.append((index, offset, live))
            chunks = jnp.maximum(chunks, (live + offset % 2 + 3) // 4)
            offset = offset + live
        reach = jnp.minimum(picks[1][1] // 2 + 2 * chunks - 1, pairs - 1)
        needed = reach // piece + 1

        def wait_piece(index, inner):
            load(index).wait()
            return inner

        lax.fori_loop(waited, needed, wait_piece, 0)
        for count in range(1, SLOTS // 4 + 2):

            @pl.when(chunks == count)
            def _(count=count):
                for pick in picks:
                    one_group(*pick, 2 * count)

        return offset, jnp.maximum(waited, needed)

    _, waited = lax.fori_loop(0, groups // 2, two_groups, (jnp.int32(0), jnp.int32(0)))

    def wait_rest(index, inner):
        load(index).wait()
        return inner

    lax.fori_loop(waited, shards, wait_rest, 0)
    keep[...] = total[:half_out]
    send[...] = total[half_out : 2 * half_out].astype(send.dtype)
    if packed_out and not packed_in:
        extra[...] = start_codes[pl.ds(me * shard_out, shard_out)]
    elif not packed_out:
        mine = offsets[me]
        parts = read_codes(me, mine, counts[order[me]], SLOT_PAIRS + 1)
        for pair, part in enumerate(shifted(parts, SLOT_PAIRS, mine % 2 == 1, True)):
            extra[pair] = part
    else:
        extra[...] = jnp.zeros(extra.shape, extra.dtype)


def gradient_call(order, counts, own, blocks, near, far, targets, packed_in, packed_out, shards):
    pairs, rows, _ = blocks[0].shape
    pairs = 2 * pairs
    groups = order.shape[0]
    half_in = near.shape[0]
    half_out = (pairs if packed_out else groups * SLOT_PAIRS) // 2
    extra = pairs // shards if packed_out else SLOT_PAIRS
    spare = SLOT_PAIRS + 2
    tile = (PATCHES, LANES)
    return pl.pallas_call(
        functools.partial(gradient_kernel, packed_in, packed_out, shards),
        grid_spec=pltpu.PrefetchScalarGridSpec(
            num_scalar_prefetch=3,
            grid=(),
            in_specs=[pl.BlockSpec(memory_space=pl.ANY)] * 4 + [pl.BlockSpec(memory_space=pltpu.VMEM)],
            out_specs=[pl.BlockSpec(memory_space=pltpu.VMEM)] * 3,
            scratch_shapes=[
                pltpu.VMEM((pairs + spare, rows, LANES), jnp.bfloat16),
                pltpu.VMEM((2 * half_in,) + tile, jnp.bfloat16),
                pltpu.VMEM((2 * half_out + spare,) + tile, jnp.float32),
                pltpu.VMEM((pairs + spare,) + tile, jnp.bfloat16),
                pltpu.SMEM((groups,), jnp.int32),
                pltpu.SemaphoreType.DMA((shards,)),
                pltpu.SemaphoreType.DMA((2,)),
            ],
        ),
        out_shape=[
            jax.ShapeDtypeStruct((half_out,) + tile, jnp.float32),
            jax.ShapeDtypeStruct((half_out,) + tile, jnp.bfloat16),
            jax.ShapeDtypeStruct((extra,) + tile, jnp.bfloat16),
        ],
        compiler_params=pltpu.CompilerParams(vmem_limit_bytes=VMEM_LIMIT),
        cost_estimate=pl.CostEstimate(
            flops=4 * pairs * rows * LANES * PATCHES, transcendentals=0, bytes_accessed=pairs * rows * LANES * 2
        ),
        name="gradient",
    )(order, counts, own, *blocks, near, far, targets)


def exchange(value, distance):
    devices = lax.axis_size("rows")
    return lax.ppermute(value, "rows", [(i, i ^ distance) for i in range(devices)])


def gather_shards(own, beside=()):
    devices = lax.axis_size("rows")
    parts = [own] + [exchange(own, 4 * k) for k in range(1, devices // 4)]
    quarter = jnp.concatenate(parts, axis=0)
    if beside:
        quarter, first = lax.optimization_barrier((quarter, beside[0]))
    near = jnp.concatenate([quarter, exchange(quarter, 2)], axis=0)
    if beside:
        near, second = lax.optimization_barrier((near, beside[1]))
        return near, exchange(near, 1), (first, second)
    return near, exchange(near, 1)


def reduce_shards(keep, send):
    devices = lax.axis_size("rows")
    half = keep + exchange(send, 1).astype(jnp.float32)
    middle = half.shape[0] // 2
    quarter = half[:middle] + exchange(half[middle:].astype(jnp.bfloat16), 2).astype(jnp.float32)
    size = quarter.shape[0] // (devices // 4)
    sent = quarter.astype(jnp.bfloat16)
    total = quarter[:size]
    for k in range(1, devices // 4):
        total = total + exchange(sent[k * size : (k + 1) * size], 4 * k).astype(jnp.float32)
    return total


def shrink(value, thresh):
    return value - jnp.clip(value, -thresh, thresh)


def local(dictionary, patches, initial_codes, support, counts, group_order, penalty):
    groups = group_order.shape[0]
    position = lax.axis_index("rows")
    devices = lax.axis_size("rows")
    momenta = momentum_list()
    owned_entries = MEAN_LIVE * groups // devices
    owned_pairs = owned_entries // 2
    pairs = owned_pairs * devices

    laid = initial_codes.reshape(SLOT_PAIRS, 2, PATCHES, BLOCK).transpose(0, 2, 1, 3)
    blocks = [collect_support(group_order, support, counts, dictionary, begin, pairs) for begin in (0, pairs)]
    near, far, blocks = gather_shards(laid.reshape(SLOT_PAIRS, PATCHES, LANES), blocks)

    own = position.astype(jnp.int32).reshape(1)
    targets = patches.T

    half_penalty = 0.5 * penalty
    ends = jnp.cumsum(jnp.take(counts, group_order))
    entry = position * owned_entries + jnp.arange(owned_entries)
    holder = jnp.sum((entry[:, None] >= ends[None, :]).astype(jnp.int32), axis=1)
    thresh = jnp.take(half_penalty, jnp.take(group_order, holder), axis=0)
    thresh = jnp.repeat(thresh.reshape(owned_pairs, 2, PATCHES).transpose(0, 2, 1), BLOCK, axis=2)
    own_thresh = lax.dynamic_index_in_dim(half_penalty, group_order[position], 0, False)[None, :, None]

    def run(near, far, packed_in, packed_out):
        return gradient_call(
            group_order, counts, own, blocks, near, far, targets, packed_in, packed_out, devices
        )

    point = previous = None
    for turn in range(ITERS - 1):
        keep, send, extra = run(near, far, turn > 0, True)
        if turn == 0:
            point = previous = extra.astype(jnp.float32)
        current = shrink(point - 0.5 * reduce_shards(keep, send), thresh)
        point = current + momenta[turn] * (current - previous)
        previous = current
        near, far = gather_shards(point.astype(jnp.bfloat16))
    keep, send, sent = run(near, far, True, False)
    result = shrink(sent.astype(jnp.float32) - 0.5 * reduce_shards(keep, send), own_thresh)
    result = result.reshape(SLOT_PAIRS, PATCHES, 2, BLOCK).transpose(0, 2, 1, 3)
    return result.reshape(1, SLOTS, PATCHES * BLOCK)


def solution(mesh):
    in_specs = (
        P("rows", None),
        P("rows", "groups"),
        P(("groups", "rows"), None, None),
        P("groups", None),
        P("groups"),
        P("groups"),
        P("groups", None),
    )
    out_specs = P(("groups", "rows"), None, None)
    return jax.shard_map(local, mesh=mesh, in_specs=in_specs, out_specs=out_specs, check_vma=False)
```

profile of v0, /device:TPU:0, one launch (start us, length us, event | category | flops | bytes accessed | tf_op | source)
XLA Modules:
  0.0 218.7 jit_solution(14168217128023372590)
XLA Ops:
  1.6 5.1 %collective-permute-start.2 = (bf16[8,64,128]{2,1,0:T(8,128)(2,1)S(1)}, bf16[8,64,128]{2,1,0:T(8,128)(2,1)S(1)}, u32[]{:S(2)}, u32[]{:S(2)}) collective-permute-start(bf16[8,64,128]{2,1,0:T(8,128)(2,1)S(1)} %reshape.124), channel_id=1, source_target_pairs={{0,12},{1,13},{2,14},{3,15},{4,8},{5,9},{6,10},{7,11},{8,4},{9,5},... | collective-permute-start | bytes 393224 | tf_op jit(solution)/shard_map/ppermute | solution.py:317
  7.4 10.3 %collect_support.2.blocks = bf16[40,512,128]{2,1,0:T(8,128)(2,1)} custom-call(s32[16]{0:T(128)} %order.9, s32[16,16]{1,0:T(8,128)} %support.3, s32[16]{0:T(128)} %counts.9, bf16[512,32768]{1,0:T(8,128)(2,1)} %dictionary.3), custom_call_target="tpu_custom_call" | custom-call | bytes 15728640 | tf_op jit(solution)/shard_map/collect_support/pallas_call | solution.py:97
  19.5 10.3 %collect_support.3.blocks_b = bf16[40,512,128]{2,1,0:T(8,128)(2,1)} custom-call(s32[16]{0:T(128)} %order.9, s32[16,16]{1,0:T(8,128)} %support.3, s32[16]{0:T(128)} %counts.9, bf16[512,32768]{1,0:T(8,128)(2,1)} %dictionary.3), custom_call_target="tpu_custom_call" | custom-call | bytes 15728640 | tf_op jit(solution)/shard_map/collect_support/pallas_call | solution.py:97
  34.8 2.5 %copy-done.2 = bf16[40,512,128]{2,1,0:T(8,128)(2,1)S(1)} copy-done((bf16[40,512,128]{2,1,0:T(8,128)(2,1)S(1)}, bf16[40,512,128]{2,1,0:T(8,128)(2,1)}, u32[]{:S(2)}) %copy-start.2) | copy-done | bytes 5242904
  37.3 2.5 %copy-done.4 = bf16[40,512,128]{2,1,0:T(8,128)(2,1)S(1)} copy-done((bf16[40,512,128]{2,1,0:T(8,128)(2,1)S(1)}, bf16[40,512,128]{2,1,0:T(8,128)(2,1)}, u32[]{:S(2)}) %copy-start.4) | copy-done | bytes 5242904
  41.0 16.6 %gradient.3 = (f32[40,64,128]{2,1,0:T(8,128)S(1)}, bf16[40,64,128]{2,1,0:T(8,128)(2,1)}, bf16[5,64,128]{2,1,0:T(8,128)(2,1)S(1)}) custom-call(s32[16]{0:T(128)S(1)} %copy-done.1, s32[16]{0:T(128)S(1)} %copy-done, s32[1]{0:T(128)} %bitcast.own, bf16[40,512,128]{2,1,0:T(8,128)(2,1)S(1)} %copy-done.2, bf16[40,512,128]{2,1,0:T(8,128)(2,1)S(1)} %copy-done.4, ...), custom_call_target="tpu_custom_call" | custom-call | flops 1342177280 | bytes 10485760 | tf_op jit(solution)/shard_map/gradient/pallas_call | solution.py:285
  63.5 7.8 %collective-permute-done.6 = bf16[20,64,128]{2,1,0:T(8,128)(2,1)S(1)} collective-permute-done((bf16[20,64,128]{2,1,0:T(8,128)(2,1)S(1)}, bf16[20,64,128]{2,1,0:T(8,128)(2,1)S(1)}, u32[]{:S(2)}, u32[]{:S(2)}) %collective-permute-start.6) | collective-permute-done | bytes 327712 | tf_op jit(solution)/shard_map/ppermute | solution.py:317
  74.1 2.4 %collective-permute-start.9 = (bf16[5,64,128]{2,1,0:T(8,128)(2,1)S(1)}, bf16[5,64,128]{2,1,0:T(8,128)(2,1)S(1)}, u32[]{:S(2)}, u32[]{:S(2)}) collective-permute-start(bf16[5,64,128]{2,1,0:T(8,128)(2,1)S(1)} %get-tuple-element.48), channel_id=1, source_target_pairs={{0,12},{1,13},{2,14},{3,15},{4,8},{5,9},{6,10},{7,11},{8,4},{9,5},... | collective-permute-start | bytes 245768 | tf_op jit(solution)/shard_map/ppermute | solution.py:317
  77.5 3.8 %collective-permute-done.9 = bf16[5,64,128]{2,1,0:T(8,128)(2,1)S(1)} collective-permute-done((bf16[5,64,128]{2,1,0:T(8,128)(2,1)S(1)}, bf16[5,64,128]{2,1,0:T(8,128)(2,1)S(1)}, u32[]{:S(2)}, u32[]{:S(2)}) %collective-permute-start.9) | collective-permute-done | bytes 81952 | tf_op jit(solution)/shard_map/ppermute | solution.py:317
  81.3 2.7 %collective-permute-done.8 = bf16[5,64,128]{2,1,0:T(8,128)(2,1)S(1)} collective-permute-done((bf16[5,64,128]{2,1,0:T(8,128)(2,1)S(1)}, bf16[5,64,128]{2,1,0:T(8,128)(2,1)S(1)}, u32[]{:S(2)}, u32[]{:S(2)}) %collective-permute-start.8) | collective-permute-done | bytes 81952 | tf_op jit(solution)/shard_map/ppermute | solution.py:317
  84.1 2.5 %collective-permute-start.12 = (bf16[5,64,128]{2,1,0:T(8,128)(2,1)S(1)}, bf16[5,64,128]{2,1,0:T(8,128)(2,1)S(1)}, u32[]{:S(2)}, u32[]{:S(2)}) collective-permute-start(bf16[5,64,128]{2,1,0:T(8,128)(2,1)S(1)} %get-tuple-element.38), channel_id=1, source_target_pairs={{0,12},{1,13},{2,14},{3,15},{4,8},{5,9},{6,10},{7,11},{8,4},{9,5},... | collective-permute-start | bytes 245768 | tf_op jit(solution)/shard_map/ppermute | solution.py:317
  88.6 2.8 %collective-permute-done.12 = bf16[5,64,128]{2,1,0:T(8,128)(2,1)S(1)} collective-permute-done((bf16[5,64,128]{2,1,0:T(8,128)(2,1)S(1)}, bf16[5,64,128]{2,1,0:T(8,128)(2,1)S(1)}, u32[]{:S(2)}, u32[]{:S(2)}) %collective-permute-start.12) | collective-permute-done | bytes 81952 | tf_op jit(solution)/shard_map/ppermute | solution.py:317
  91.4 2.0 collective-permute-done.11
  95.1 7.6 %collective-permute-done.13 = bf16[20,64,128]{2,1,0:T(8,128)(2,1)S(1)} collective-permute-done((bf16[20,64,128]{2,1,0:T(8,128)(2,1)S(1)}, bf16[20,64,128]{2,1,0:T(8,128)(2,1)S(1)}, u32[]{:S(2)}, u32[]{:S(2)}) %collective-permute-start.13) | collective-permute-done | bytes 327712 | tf_op jit(solution)/shard_map/ppermute | solution.py:317
  102.9 2.1 collective-permute-done.14.far
  104.9 2.5 %copy-done.3 = bf16[40,512,128]{2,1,0:T(8,128)(2,1)S(1)} copy-done((bf16[40,512,128]{2,1,0:T(8,128)(2,1)S(1)}, bf16[40,512,128]{2,1,0:T(8,128)(2,1)}, u32[]{:S(2)}) %copy-start.3) | copy-done | bytes 5242904
  107.4 2.5 %copy-done.5 = bf16[40,512,128]{2,1,0:T(8,128)(2,1)S(1)} copy-done((bf16[40,512,128]{2,1,0:T(8,128)(2,1)S(1)}, bf16[40,512,128]{2,1,0:T(8,128)(2,1)}, u32[]{:S(2)}) %copy-start.5) | copy-done | bytes 5242904
  109.9 15.8 %gradient.4 = (f32[40,64,128]{2,1,0:T(8,128)S(1)}, bf16[40,64,128]{2,1,0:T(8,128)(2,1)S(1)}, bf16[5,64,128]{2,1,0:T(8,128)(2,1)}) custom-call(s32[16]{0:T(128)S(1)} %copy-done.1, s32[16]{0:T(128)S(1)} %copy-done, s32[1]{0:T(128)} %bitcast.own, bf16[40,512,128]{2,1,0:T(8,128)(2,1)S(1)} %copy-done.3, bf16[40,512,128]{2,1,0:T(8,128)(2,1)S(1)} %copy-done.5, ...), custom_call_target="tpu_custom_call" | custom-call | flops 1342177280 | bytes 10485760 | tf_op jit(solution)/shard_map/gradient/pallas_call | solution.py:285
  129.7 8.2 %collective-permute-done.16 = bf16[20,64,128]{2,1,0:T(8,128)(2,1)S(1)} collective-permute-done((bf16[20,64,128]{2,1,0:T(8,128)(2,1)S(1)}, bf16[20,64,128]{2,1,0:T(8,128)(2,1)S(1)}, u32[]{:S(2)}, u32[]{:S(2)}) %collective-permute-start.16) | collective-permute-done | bytes 327712 | tf_op jit(solution)/shard_map/ppermute | solution.py:317
  138.2 2.4 %collective-permute-start.19 = (bf16[5,64,128]{2,1,0:T(8,128)(2,1)S(1)}, bf16[5,64,128]{2,1,0:T(8,128)(2,1)S(1)}, u32[]{:S(2)}, u32[]{:S(2)}) collective-permute-start(bf16[5,64,128]{2,1,0:T(8,128)(2,1)S(1)} %get-tuple-element.45), channel_id=1, source_target_pairs={{0,12},{1,13},{2,14},{3,15},{4,8},{5,9},{6,10},{7,11},{8,4},{9,5},... | collective-permute-start | bytes 245768 | tf_op jit(solution)/shard_map/ppermute | solution.py:317
  145.5 3.2 %collective-permute-done.18 = bf16[5,64,128]{2,1,0:T(8,128)(2,1)S(1)} collective-permute-done((bf16[5,64,128]{2,1,0:T(8,128)(2,1)S(1)}, bf16[5,64,128]{2,1,0:T(8,128)(2,1)S(1)}, u32[]{:S(2)}, u32[]{:S(2)}) %collective-permute-start.18) | collective-permute-done | bytes 81952 | tf_op jit(solution)/shard_map/ppermute | solution.py:317
  148.8 2.1 collective-permute-start.22
  150.9 2.4 %collective-permute-start.20 = (bf16[5,64,128]{2,1,0:T(8,128)(2,1)S(1)}, bf16[5,64,128]{2,1,0:T(8,128)(2,1)S(1)}, u32[]{:S(2)}, u32[]{:S(2)}) collective-permute-start(bf16[5,64,128]{2,1,0:T(8,128)(2,1)S(1)} %get-tuple-element.34), channel_id=1, source_target_pairs={{0,4},{1,5},{2,6},{3,7},{4,0},{5,1},{6,2},{7,3},{8,12},{9,13},{10,... | collective-permute-start | bytes 245768 | tf_op jit(solution)/shard_map/ppermute | solution.py:317
  153.3 2.8 %collective-permute-done.22 = bf16[5,64,128]{2,1,0:T(8,128)(2,1)S(1)} collective-permute-done((bf16[5,64,128]{2,1,0:T(8,128)(2,1)S(1)}, bf16[5,64,128]{2,1,0:T(8,128)(2,1)S(1)}, u32[]{:S(2)}, u32[]{:S(2)}) %collective-permute-start.22) | collective-permute-done | bytes 81952 | tf_op jit(solution)/shard_map/ppermute | solution.py:317
  159.4 7.5 %collective-permute-done.23 = bf16[20,64,128]{2,1,0:T(8,128)(2,1)S(1)} collective-permute-done((bf16[20,64,128]{2,1,0:T(8,128)(2,1)S(1)}, bf16[20,64,128]{2,1,0:T(8,128)(2,1)S(1)}, u32[]{:S(2)}, u32[]{:S(2)}) %collective-permute-start.23) | collective-permute-done | bytes 327712 | tf_op jit(solution)/shard_map/ppermute | solution.py:317
  167.0 2.1 collective-permute-done.24.far
  169.1 16.2 %gradient.5 = (f32[64,64,128]{2,1,0:T(8,128)S(1)}, bf16[64,64,128]{2,1,0:T(8,128)(2,1)S(1)}, bf16[8,64,128]{2,1,0:T(8,128)(2,1)S(1)}) custom-call(s32[16]{0:T(128)S(1)} %copy-done.1, s32[16]{0:T(128)S(1)} %copy-done, s32[1]{0:T(128)} %bitcast.own, bf16[40,512,128]{2,1,0:T(8,128)(2,1)S(1)} %copy-done.3, bf16[40,512,128]{2,1,0:T(8,128)(2,1)S(1)} %copy-done.5, ...), custom_call_target="tpu_custom_call" | custom-call | flops 1342177280 | bytes 10485760 | tf_op jit(solution)/shard_map/gradient/pallas_call | solution.py:285
  185.6 2.5 %collective-permute-done.25 = bf16[64,64,128]{2,1,0:T(8,128)(2,1)S(1)} collective-permute-done((bf16[64,64,128]{2,1,0:T(8,128)(2,1)S(1)}, bf16[64,64,128]{2,1,0:T(8,128)(2,1)S(1)}, u32[]{:S(2)}, u32[]{:S(2)}) %collective-permute-start.25) | collective-permute-done | bytes 1048608 | tf_op jit(solution)/shard_map/ppermute | solution.py:317
  190.2 12.5 %collective-permute-done.26 = bf16[32,64,128]{2,1,0:T(8,128)(2,1)S(1)} collective-permute-done((bf16[32,64,128]{2,1,0:T(8,128)(2,1)S(1)}, bf16[32,64,128]{2,1,0:T(8,128)(2,1)S(1)}, u32[]{:S(2)}, u32[]{:S(2)}) %collective-permute-start.26) | collective-permute-done | bytes 524320 | tf_op jit(solution)/shard_map/ppermute | solution.py:317
  203.0 2.2 collective-permute-start.29
  209.9 2.4 %collective-permute-done.29 = bf16[8,64,128]{2,1,0:T(8,128)(2,1)S(1)} collective-permute-done((bf16[8,64,128]{2,1,0:T(8,128)(2,1)S(1)}, bf16[8,64,128]{2,1,0:T(8,128)(2,1)S(1)}, u32[]{:S(2)}, u32[]{:S(2)}) %collective-permute-start.29) | collective-permute-done | bytes 131104 | tf_op jit(solution)/shard_map/ppermute | solution.py:317
  212.2 5.0 %collective-permute-done.28 = bf16[8,64,128]{2,1,0:T(8,128)(2,1)S(1)} collective-permute-done((bf16[8,64,128]{2,1,0:T(8,128)(2,1)S(1)}, bf16[8,64,128]{2,1,0:T(8,128)(2,1)S(1)}, u32[]{:S(2)}, u32[]{:S(2)}) %collective-permute-start.28) | collective-permute-done | bytes 131104 | tf_op jit(solution)/shard_map/ppermute | solution.py:317
  (113 shorter events, 43.1 us)
Async XLA Ops:
  1.6 16.1 %collective-permute-start.2 = (bf16[8,64,128]{2,1,0:T(8,128)(2,1)S(1)}, bf16[8,64,128]{2,1,0:T(8,128)(2,1)S(1)}, u32[]{:S(2)}, u32[]{:S(2)}) collective-permute-start(bf16[8,64,128]{2,1,0:T(8,128)(2,1)S(1)} %reshape.124), channel_id=1, source_target_pairs={{0,12},{1,13},{2,14},{3,15},{4,8},{5,9},{6,10},{7,11},{8,4},{9,5},... | collective-permute-start | bytes 393224 | tf_op jit(solution)/shard_map/ppermute | solution.py:317
  6.7 11.1 %collective-permute-start.1 = (bf16[8,64,128]{2,1,0:T(8,128)(2,1)S(1)}, bf16[8,64,128]{2,1,0:T(8,128)(2,1)S(1)}, u32[]{:S(2)}, u32[]{:S(2)}) collective-permute-start(bf16[8,64,128]{2,1,0:T(8,128)(2,1)S(1)} %reshape.124), channel_id=1, source_target_pairs={{0,8},{1,9},{2,10},{3,11},{4,12},{5,13},{6,14},{7,15},{8,0},{9,1},... | collective-permute-start | bytes 393224 | tf_op jit(solution)/shard_map/ppermute | solution.py:317
  6.7 11.1 %collective-permute-start = (bf16[8,64,128]{2,1,0:T(8,128)(2,1)S(1)}, bf16[8,64,128]{2,1,0:T(8,128)(2,1)S(1)}, u32[]{:S(2)}, u32[]{:S(2)}) collective-permute-start(bf16[8,64,128]{2,1,0:T(8,128)(2,1)S(1)} %reshape.124), channel_id=1, source_target_pairs={{0,4},{1,5},{2,6},{3,7},{4,0},{5,1},{6,2},{7,3},{8,12},{9,13},{10,... | collective-permute-start | bytes 393224 | tf_op jit(solution)/shard_map/ppermute | solution.py:317
  17.9 13.1 %collective-permute-start.3 = (bf16[32,64,128]{2,1,0:T(8,128)(2,1)S(1)}, bf16[32,64,128]{2,1,0:T(8,128)(2,1)S(1)}, u32[]{:S(2)}, u32[]{:S(2)}) collective-permute-start(bf16[32,64,128]{2,1,0:T(8,128)(2,1)S(1)} %pad_maximum_fusion.1), channel_id=1, source_target_pairs={{0,2},{1,3},{2,0},{3,1},{4,6},{5,7},{6,4},{7,5},{8,10},{9,11},{10,... | collective-permute-start | bytes 1572872 | tf_op jit(solution)/shard_map/ppermute | solution.py:317
  31.1 2.7 %collective-permute-start.4 = (bf16[64,64,128]{2,1,0:T(8,128)(2,1)S(1)}, bf16[64,64,128]{2,1,0:T(8,128)(2,1)S(1)}, u32[]{:S(2)}, u32[]{:S(2)}) collective-permute-start(bf16[64,64,128]{2,1,0:T(8,128)(2,1)S(1)} %pad_maximum_fusion.near), channel_id=1, source_target_pairs={{0,1},{1,0},{2,3},{3,2},{4,5},{5,4},{6,7},{7,6},{8,9},{9,8},{10,11... | collective-permute-start | bytes 3145736 | tf_op jit(solution)/shard_map/ppermute | solution.py:317
  41.0 18.0 %copy-start.9 = (f32[16,64]{1,0:T(8,128)S(1)}, f32[16,64]{1,0:T(8,128)}, u32[]{:S(2)}) copy-start(f32[16,64]{1,0:T(8,128)} %param.13) | copy-start | bytes 12292
  57.6 2.5 %collective-permute-start.5 = (bf16[40,64,128]{2,1,0:T(8,128)(2,1)}, bf16[40,64,128]{2,1,0:T(8,128)(2,1)S(1)}, u32[]{:S(2)}, u32[]{:S(2)}) collective-permute-start(bf16[40,64,128]{2,1,0:T(8,128)(2,1)} %get-tuple-element.23), channel_id=1, source_target_pairs={{0,1},{1,0},{2,3},{3,2},{4,5},{5,4},{6,7},{7,6},{8,9},{9,8},{10,11... | collective-permute-start | bytes 1966088 | tf_op jit(solution)/shard_map/ppermute | solution.py:317
  61.3 10.1 %collective-permute-start.6 = (bf16[20,64,128]{2,1,0:T(8,128)(2,1)S(1)}, bf16[20,64,128]{2,1,0:T(8,128)(2,1)S(1)}, u32[]{:S(2)}, u32[]{:S(2)}) collective-permute-start(bf16[20,64,128]{2,1,0:T(8,128)(2,1)S(1)} %slice.144), channel_id=1, source_target_pairs={{0,2},{1,3},{2,0},{3,1},{4,6},{5,7},{6,4},{7,5},{8,10},{9,11},{10,... | collective-permute-start | bytes 983048 | tf_op jit(solution)/shard_map/ppermute | solution.py:317
  72.6 4.9 %collective-permute-start.7 = (bf16[5,64,128]{2,1,0:T(8,128)(2,1)S(1)}, bf16[5,64,128]{2,1,0:T(8,128)(2,1)S(1)}, u32[]{:S(2)}, u32[]{:S(2)}) collective-permute-start(bf16[5,64,128]{2,1,0:T(8,128)(2,1)S(1)} %get-tuple-element.47), channel_id=1, source_target_pairs={{0,4},{1,5},{2,6},{3,7},{4,0},{5,1},{6,2},{7,3},{8,12},{9,13},{10,... | collective-permute-start | bytes 245768 | tf_op jit(solution)/shard_map/ppermute | solution.py:317
  74.1 7.3 %collective-permute-start.9 = (bf16[5,64,128]{2,1,0:T(8,128)(2,1)S(1)}, bf16[5,64,128]{2,1,0:T(8,128)(2,1)S(1)}, u32[]{:S(2)}, u32[]{:S(2)}) collective-permute-start(bf16[5,64,128]{2,1,0:T(8,128)(2,1)S(1)} %get-tuple-element.48), channel_id=1, source_target_pairs={{0,12},{1,13},{2,14},{3,15},{4,8},{5,9},{6,10},{7,11},{8,4},{9,5},... | collective-permute-start | bytes 245768 | tf_op jit(solution)/shard_map/ppermute | solution.py:317
  76.4 7.6 %collective-permute-start.8 = (bf16[5,64,128]{2,1,0:T(8,128)(2,1)S(1)}, bf16[5,64,128]{2,1,0:T(8,128)(2,1)S(1)}, u32[]{:S(2)}, u32[]{:S(2)}) collective-permute-start(bf16[5,64,128]{2,1,0:T(8,128)(2,1)S(1)} %get-tuple-element.49), channel_id=1, source_target_pairs={{0,8},{1,9},{2,10},{3,11},{4,12},{5,13},{6,14},{7,15},{8,0},{9,1},... | collective-permute-start | bytes 245768 | tf_op jit(solution)/shard_map/ppermute | solution.py:317
  84.1 7.3 %collective-permute-start.12 = (bf16[5,64,128]{2,1,0:T(8,128)(2,1)S(1)}, bf16[5,64,128]{2,1,0:T(8,128)(2,1)S(1)}, u32[]{:S(2)}, u32[]{:S(2)}) collective-permute-start(bf16[5,64,128]{2,1,0:T(8,128)(2,1)S(1)} %get-tuple-element.38), channel_id=1, source_target_pairs={{0,12},{1,13},{2,14},{3,15},{4,8},{5,9},{6,10},{7,11},{8,4},{9,5},... | collective-permute-start | bytes 245768 | tf_op jit(solution)/shard_map/ppermute | solution.py:317
  86.7 6.7 %collective-permute-start.11 = (bf16[5,64,128]{2,1,0:T(8,128)(2,1)S(1)}, bf16[5,64,128]{2,1,0:T(8,128)(2,1)S(1)}, u32[]{:S(2)}, u32[]{:S(2)}) collective-permute-start(bf16[5,64,128]{2,1,0:T(8,128)(2,1)S(1)} %get-tuple-element.38), channel_id=1, source_target_pairs={{0,8},{1,9},{2,10},{3,11},{4,12},{5,13},{6,14},{7,15},{8,0},{9,1},... | collective-permute-start | bytes 245768 | tf_op jit(solution)/shard_map/ppermute | solution.py:317
  86.7 6.7 %collective-permute-start.10 = (bf16[5,64,128]{2,1,0:T(8,128)(2,1)S(1)}, bf16[5,64,128]{2,1,0:T(8,128)(2,1)S(1)}, u32[]{:S(2)}, u32[]{:S(2)}) collective-permute-start(bf16[5,64,128]{2,1,0:T(8,128)(2,1)S(1)} %get-tuple-element.38), channel_id=1, source_target_pairs={{0,4},{1,5},{2,6},{3,7},{4,0},{5,1},{6,2},{7,3},{8,12},{9,13},{10,... | collective-permute-start | bytes 245768 | tf_op jit(solution)/shard_map/ppermute | solution.py:317
  93.5 9.3 %collective-permute-start.13 = (bf16[20,64,128]{2,1,0:T(8,128)(2,1)S(1)}, bf16[20,64,128]{2,1,0:T(8,128)(2,1)S(1)}, u32[]{:S(2)}, u32[]{:S(2)}) collective-permute-start(bf16[20,64,128]{2,1,0:T(8,128)(2,1)S(1)} %pad_maximum_fusion.2), channel_id=1, source_target_pairs={{0,2},{1,3},{2,0},{3,1},{4,6},{5,7},{6,4},{7,5},{8,10},{9,11},{10,... | collective-permute-start | bytes 983048 | tf_op jit(solution)/shard_map/ppermute | solution.py:317
  102.8 2.2 collective-permute-start.14
  104.9 2.5 %copy-start.3 = (bf16[40,512,128]{2,1,0:T(8,128)(2,1)S(1)}, bf16[40,512,128]{2,1,0:T(8,128)(2,1)}, u32[]{:S(2)}) copy-start(bf16[40,512,128]{2,1,0:T(8,128)(2,1)} %collect_support.2.blocks) | copy-start | bytes 15728644
  125.7 2.2 collective-permute-start.15
  128.1 9.8 %collective-permute-start.16 = (bf16[20,64,128]{2,1,0:T(8,128)(2,1)S(1)}, bf16[20,64,128]{2,1,0:T(8,128)(2,1)S(1)}, u32[]{:S(2)}, u32[]{:S(2)}) collective-permute-start(bf16[20,64,128]{2,1,0:T(8,128)(2,1)S(1)} %slice.143), channel_id=1, source_target_pairs={{0,2},{1,3},{2,0},{3,1},{4,6},{5,7},{6,4},{7,5},{8,10},{9,11},{10,... | collective-permute-start | bytes 983048 | tf_op jit(solution)/shard_map/ppermute | solution.py:317
  138.1 5.5 %collective-permute-start.17 = (bf16[5,64,128]{2,1,0:T(8,128)(2,1)S(1)}, bf16[5,64,128]{2,1,0:T(8,128)(2,1)S(1)}, u32[]{:S(2)}, u32[]{:S(2)}) collective-permute-start(bf16[5,64,128]{2,1,0:T(8,128)(2,1)S(1)} %get-tuple-element.44), channel_id=1, source_target_pairs={{0,4},{1,5},{2,6},{3,7},{4,0},{5,1},{6,2},{7,3},{8,12},{9,13},{10,... | collective-permute-start | bytes 245768 | tf_op jit(solution)/shard_map/ppermute | solution.py:317
  138.2 7.3 %collective-permute-start.19 = (bf16[5,64,128]{2,1,0:T(8,128)(2,1)S(1)}, bf16[5,64,128]{2,1,0:T(8,128)(2,1)S(1)}, u32[]{:S(2)}, u32[]{:S(2)}) collective-permute-start(bf16[5,64,128]{2,1,0:T(8,128)(2,1)S(1)} %get-tuple-element.45), channel_id=1, source_target_pairs={{0,12},{1,13},{2,14},{3,15},{4,8},{5,9},{6,10},{7,11},{8,4},{9,5},... | collective-permute-start | bytes 245768 | tf_op jit(solution)/shard_map/ppermute | solution.py:317
  140.6 8.0 %collective-permute-start.18 = (bf16[5,64,128]{2,1,0:T(8,128)(2,1)S(1)}, bf16[5,64,128]{2,1,0:T(8,128)(2,1)S(1)}, u32[]{:S(2)}, u32[]{:S(2)}) collective-permute-start(bf16[5,64,128]{2,1,0:T(8,128)(2,1)S(1)} %get-tuple-element.46), channel_id=1, source_target_pairs={{0,8},{1,9},{2,10},{3,11},{4,12},{5,13},{6,14},{7,15},{8,0},{9,1},... | collective-permute-start | bytes 245768 | tf_op jit(solution)/shard_map/ppermute | solution.py:317
  148.8 7.2 %collective-permute-start.22 = (bf16[5,64,128]{2,1,0:T(8,128)(2,1)S(1)}, bf16[5,64,128]{2,1,0:T(8,128)(2,1)S(1)}, u32[]{:S(2)}, u32[]{:S(2)}) collective-permute-start(bf16[5,64,128]{2,1,0:T(8,128)(2,1)S(1)} %get-tuple-element.34), channel_id=1, source_target_pairs={{0,12},{1,13},{2,14},{3,15},{4,8},{5,9},{6,10},{7,11},{8,4},{9,5},... | collective-permute-start | bytes 245768 | tf_op jit(solution)/shard_map/ppermute | solution.py:317
  150.9 6.8 %collective-permute-start.21 = (bf16[5,64,128]{2,1,0:T(8,128)(2,1)S(1)}, bf16[5,64,128]{2,1,0:T(8,128)(2,1)S(1)}, u32[]{:S(2)}, u32[]{:S(2)}) collective-permute-start(bf16[5,64,128]{2,1,0:T(8,128)(2,1)S(1)} %get-tuple-element.34), channel_id=1, source_target_pairs={{0,8},{1,9},{2,10},{3,11},{4,12},{5,13},{6,14},{7,15},{8,0},{9,1},... | collective-permute-start | bytes 245768 | tf_op jit(solution)/shard_map/ppermute | solution.py:317
  150.9 6.8 %collective-permute-start.20 = (bf16[5,64,128]{2,1,0:T(8,128)(2,1)S(1)}, bf16[5,64,128]{2,1,0:T(8,128)(2,1)S(1)}, u32[]{:S(2)}, u32[]{:S(2)}) collective-permute-start(bf16[5,64,128]{2,1,0:T(8,128)(2,1)S(1)} %get-tuple-element.34), channel_id=1, source_target_pairs={{0,4},{1,5},{2,6},{3,7},{4,0},{5,1},{6,2},{7,3},{8,12},{9,13},{10,... | collective-permute-start | bytes 245768 | tf_op jit(solution)/shard_map/ppermute | solution.py:317
  157.8 9.1 %collective-permute-start.23 = (bf16[20,64,128]{2,1,0:T(8,128)(2,1)S(1)}, bf16[20,64,128]{2,1,0:T(8,128)(2,1)S(1)}, u32[]{:S(2)}, u32[]{:S(2)}) collective-permute-start(bf16[20,64,128]{2,1,0:T(8,128)(2,1)S(1)} %pad_maximum_fusion.3), channel_id=1, source_target_pairs={{0,2},{1,3},{2,0},{3,1},{4,6},{5,7},{6,4},{7,5},{8,10},{9,11},{10,... | collective-permute-start | bytes 983048 | tf_op jit(solution)/shard_map/ppermute | solution.py:317
  167.0 2.2 collective-permute-start.24
  185.4 2.7 %collective-permute-start.25 = (bf16[64,64,128]{2,1,0:T(8,128)(2,1)S(1)}, bf16[64,64,128]{2,1,0:T(8,128)(2,1)S(1)}, u32[]{:S(2)}, u32[]{:S(2)}) collective-permute-start(bf16[64,64,128]{2,1,0:T(8,128)(2,1)S(1)} %get-tuple-element.28), channel_id=1, source_target_pairs={{0,1},{1,0},{2,3},{3,2},{4,5},{5,4},{6,7},{7,6},{8,9},{9,8},{10,11... | collective-permute-start | bytes 3145736 | tf_op jit(solution)/shard_map/ppermute | solution.py:317
  188.6 14.0 %collective-permute-start.26 = (bf16[32,64,128]{2,1,0:T(8,128)(2,1)S(1)}, bf16[32,64,128]{2,1,0:T(8,128)(2,1)S(1)}, u32[]{:S(2)}, u32[]{:S(2)}) collective-permute-start(bf16[32,64,128]{2,1,0:T(8,128)(2,1)S(1)} %slice.142), channel_id=1, source_target_pairs={{0,2},{1,3},{2,0},{3,1},{4,6},{5,7},{6,4},{7,5},{8,10},{9,11},{10,... | collective-permute-start | bytes 1572872 | tf_op jit(solution)/shard_map/ppermute | solution.py:317
  202.9 7.0 %collective-permute-start.27 = (bf16[8,64,128]{2,1,0:T(8,128)(2,1)S(1)}, bf16[8,64,128]{2,1,0:T(8,128)(2,1)S(1)}, u32[]{:S(2)}, u32[]{:S(2)}) collective-permute-start(bf16[8,64,128]{2,1,0:T(8,128)(2,1)S(1)} %get-tuple-element.41), channel_id=1, source_target_pairs={{0,4},{1,5},{2,6},{3,7},{4,0},{5,1},{6,2},{7,3},{8,12},{9,13},{10,... | collective-permute-start | bytes 393224 | tf_op jit(solution)/shard_map/ppermute | solution.py:317
  203.0 9.3 %collective-permute-start.29 = (bf16[8,64,128]{2,1,0:T(8,128)(2,1)S(1)}, bf16[8,64,128]{2,1,0:T(8,128)(2,1)S(1)}, u32[]{:S(2)}, u32[]{:S(2)}) collective-permute-start(bf16[8,64,128]{2,1,0:T(8,128)(2,1)S(1)} %get-tuple-element.42), channel_id=1, source_target_pairs={{0,12},{1,13},{2,14},{3,15},{4,8},{5,9},{6,10},{7,11},{8,4},{9,5},... | collective-permute-start | bytes 393224 | tf_op jit(solution)/shard_map/ppermute | solution.py:317
  205.1 12.1 %collective-permute-start.28 = (bf16[8,64,128]{2,1,0:T(8,128)(2,1)S(1)}, bf16[8,64,128]{2,1,0:T(8,128)(2,1)S(1)}, u32[]{:S(2)}, u32[]{:S(2)}) collective-permute-start(bf16[8,64,128]{2,1,0:T(8,128)(2,1)S(1)} %get-tuple-element.43), channel_id=1, source_target_pairs={{0,8},{1,9},{2,10},{3,11},{4,12},{5,13},{6,14},{7,15},{8,0},{9,1},... | collective-permute-start | bytes 393224 | tf_op jit(solution)/shard_map/ppermute | solution.py:317
  (8 other events, 13.3 us)
where the time goes:
time: 218 us; the launch traced here: 219 us
  waiting for transfers between devices  85.6 us (39%)
  Pallas kernels  69.2 us (32%)
  starting transfers between devices  36.6 us (17%)
  local copies, waits for them, and re-layouts  21.4 us (10%)
  other arithmetic  3.46 us (2%)
  between operations  2.41 us (1%)
    ppermute x30, waiting for transfers between devices, exchange(): lax.ppermute(value, 'rows', [(i, i ^ distance) for i in range(devices)])  85.6 us
    pallas_call x3, Pallas kernels, gradient_call(): pl.pallas_call(functools.partial(gradient_kernel, packed_in, packed_out,...  48.6 us
    ppermute x30, starting transfers between devices, exchange(): lax.ppermute(value, 'rows', [(i, i ^ distance) for i in range(devices)])  36.6 us
    pallas_call x2, Pallas kernels, collect_support(): pl.pallas_call(functools.partial(support_kernel, begin), grid_spec=pltpu....  20.6 us
    unnamed x27, local copies, waits for them, and re-layouts  14.8 us
  transfers between devices with their start and end apart: 30, of which 24 were waited for; matrix products, arithmetic and copies ran while one was open for 3% of the time, Pallas kernels for 9%

commit v1 on v0

--- a/solution.py
+++ b/solution.py
@@ -14,8 +14,7 @@
 MEAN_LIVE = 10
 LANES = 2 * BLOCK
 SLOT_PAIRS = SLOTS // 2
-VMEM_LIMIT = 32 * 1024 * 1024
-SUPPORT_VMEM = 58 * 1024 * 1024
+VMEM_LIMIT = 60 * 1024 * 1024
 
 
 def momentum_list():
@@ -110,7 +109,7 @@
             ],
         ),
         out_shape=jax.ShapeDtypeStruct((pairs, rows, LANES), dictionary.dtype),
-        compiler_params=pltpu.CompilerParams(vmem_limit_bytes=SUPPORT_VMEM),
+        compiler_params=pltpu.CompilerParams(vmem_limit_bytes=VMEM_LIMIT),
         cost_estimate=pl.CostEstimate(
             flops=0, transcendentals=0, bytes_accessed=3 * pairs * rows * LANES * 2
         ),
@@ -120,7 +119,7 @@
 
 def relative_slot(index, me, devices):
     apart = index ^ me
-    return (apart % 2) * (devices // 2) + ((apart // 2) % 2) * (devices // 4) + apart // 4
+    return (apart % 2) * (devices // 2) + ((apart // 2) % 2) * (devices // 4) + index // 4
 
 
 def gradient_kernel(
@@ -317,10 +316,15 @@
     return lax.ppermute(value, "rows", [(i, i ^ distance) for i in range(devices)])
 
 
+def trade(value):
+    columns = lax.axis_size("rows") // 4
+    groups = [[4 * i + rest for i in range(columns)] for rest in range(4)]
+    return lax.all_to_all(value, "rows", 0, 0, axis_index_groups=groups, tiled=True)
+
+
 def gather_shards(own, beside=()):
     devices = lax.axis_size("rows")
-    parts = [own] + [exchange(own, 4 * k) for k in range(1, devices // 4)]
-    quarter = jnp.concatenate(parts, axis=0)
+    quarter = trade(jnp.concatenate([own] * (devices // 4), axis=0))
     if beside:
         quarter, first = lax.optimization_barrier((quarter, beside[0]))
     near = jnp.concatenate([quarter, exchange(quarter, 2)], axis=0)
@@ -335,12 +339,8 @@
     half = keep + exchange(send, 1).astype(jnp.float32)
     middle = half.shape[0] // 2
     quarter = half[:middle] + exchange(half[middle:].astype(jnp.bfloat16), 2).astype(jnp.float32)
-    size = quarter.shape[0] // (devices // 4)
-    sent = quarter.astype(jnp.bfloat16)
-    total = quarter[:size]
-    for k in range(1, devices // 4):
-        total = total + exchange(sent[k * size : (k + 1) * size], 4 * k).astype(jnp.float32)
-    return total
+    shares = trade(quarter.astype(jnp.bfloat16)).astype(jnp.float32)
+    return jnp.sum(shares.reshape((devices // 4, -1) + shares.shape[1:]), axis=0)
 
 
 def shrink(value, thresh):

time: 218 us -> 237 us (1.087)
  blocking collectives: 0 us -> 37 us
  starting transfers between devices: 36.6 us -> 23.8 us
  local copies, waits for them, and re-layouts: 21.4 us -> 9.73 us
  Pallas kernels: 69.2 us -> 78.7 us
  waiting for transfers between devices: 85.6 us -> 77.2 us
  other arithmetic: 3.46 us -> 8.78 us
    all_to_all x0 -> x3, blocking collectives: none -> 37 us  [trade(): lax.all_to_all(value, 'rows', 0, 0, axis_index_groups=groups, tiled=True)]
    ppermute x30 -> x12, waiting for transfers between devices: 85.6 us -> 53 us  [exchange(): lax.ppermute(value, 'rows', [(i, i ^ distance) for i in range(devices)])]
    ppermute x30 -> x12, starting transfers between devices: 36.6 us -> 10.2 us  [exchange(): lax.ppermute(value, 'rows', [(i, i ^ distance) for i in range(devices)])]
    all_to_all x0 -> x3, waiting for transfers between devices: none -> 24.1 us  [trade(): lax.all_to_all(value, 'rows', 0, 0, axis_index_groups=groups, tiled=True)]
    all_to_all x0 -> x3, starting transfers between devices: none -> 13.7 us  [trade(): lax.all_to_all(value, 'rows', 0, 0, axis_index_groups=groups, tiled=True)]
    unnamed x27 -> x29, local copies, waits for them, and re-layouts: 14.8 us -> 3.14 us
    pallas_call x3, Pallas kernels: 48.6 us -> 58.1 us  [gradient_call(): pl.pallas_call(functools.partial(gradient_kernel, packed_in, packed_out,...]
    add x3, other arithmetic: 0.76 us -> 4.91 us  [reduce_shards(): half = keep + exchange(send, 1).astype(jnp.float32)]
  transfers between devices with their start and end apart: 30 -> 15, of which waited for: 24 -> 15; matrix products, arithmetic and copies ran while one was open for 3% -> 2% of each run, Pallas kernels for 9% -> 9%
where the time goes in v1:
time: 237 us; the launch traced here: 238 us
  Pallas kernels  78.7 us (33%)
  waiting for transfers between devices  77.2 us (33%)
  blocking collectives  37 us (16%)
  starting transfers between devices  23.8 us (10%)
  local copies, waits for them, and re-layouts  9.73 us (4%)
  other arithmetic  8.78 us (4%)
    pallas_call x3, Pallas kernels, gradient_call(): pl.pallas_call(functools.partial(gradient_kernel, packed_in, packed_out,...  58.1 us
    ppermute x12, waiting for transfers between devices, exchange(): lax.ppermute(value, 'rows', [(i, i ^ distance) for i in range(devices)])  53 us
    all_to_all x3, blocking collectives, trade(): lax.all_to_all(value, 'rows', 0, 0, axis_index_groups=groups, tiled=True)  37 us
    all_to_all x3, waiting for transfers between devices, trade(): lax.all_to_all(value, 'rows', 0, 0, axis_index_groups=groups, tiled=True)  24.1 us
    pallas_call x2, Pallas kernels, collect_support(): pl.pallas_call(functools.partial(support_kernel, begin), grid_spec=pltpu....  20.6 us
    all_to_all x3, starting transfers between devices, trade(): lax.all_to_all(value, 'rows', 0, 0, axis_index_groups=groups, tiled=True)  13.7 us
    ppermute x12, starting transfers between devices, exchange(): lax.ppermute(value, 'rows', [(i, i ^ distance) for i in range(devices)])  10.2 us
    add x3, other arithmetic, reduce_shards(): half = keep + exchange(send, 1).astype(jnp.float32)  4.91 us
  transfers between devices with their start and end apart: 15, of which 15 were waited for; matrix products, arithmetic and copies ran while one was open for 2% of the time, Pallas kernels for 9%

profile of v1, /device:TPU:0, one launch (start us, length us, event | category | flops | bytes accessed | tf_op | source)
XLA Modules:
  0.0 237.5 jit_solution(13428754184706348511)
XLA Ops:
  2.5 6.3 %all-to-all-start = ((bf16[32,64,128]{2,1,0:T(8,128)(2,1)}), bf16[32,64,128]{2,1,0:T(8,128)(2,1)S(1)}, u32[]{:S(2)}, u32[]{:S(2)}) async-start(bf16[32,64,128]{2,1,0:T(8,128)(2,1)} %pad_maximum_fusion.1), calls=%async_computation | async-start | bytes 1048576 | tf_op jit(solution)/shard_map/all_to_all | solution.py:322
  8.8 10.3 %collect_support.2.blocks = bf16[40,512,128]{2,1,0:T(8,128)(2,1)} custom-call(s32[16]{0:T(128)} %order.9, s32[16,16]{1,0:T(8,128)} %support.3, s32[16]{0:T(128)} %counts.9, bf16[512,32768]{1,0:T(8,128)(2,1)} %dictionary.3), custom_call_target="tpu_custom_call" | custom-call | bytes 15728640 | tf_op jit(solution)/shard_map/collect_support/pallas_call | solution.py:96
  19.1 4.2 %all-to-all-done = bf16[32,64,128]{2,1,0:T(8,128)(2,1)S(1)} async-done(((bf16[32,64,128]{2,1,0:T(8,128)(2,1)}), bf16[32,64,128]{2,1,0:T(8,128)(2,1)S(1)}, u32[]{:S(2)}, u32[]{:S(2)}) %all-to-all-start) | async-done | bytes 524320 | tf_op jit(solution)/shard_map/all_to_all | solution.py:322
  23.3 1.5 collective-permute-start
  24.8 10.3 %collect_support.3.blocks_b = bf16[40,512,128]{2,1,0:T(8,128)(2,1)} custom-call(s32[16]{0:T(128)} %order.9, s32[16,16]{1,0:T(8,128)} %support.3, s32[16]{0:T(128)} %counts.9, bf16[512,32768]{1,0:T(8,128)(2,1)} %dictionary.3), custom_call_target="tpu_custom_call" | custom-call | bytes 15728640 | tf_op jit(solution)/shard_map/collect_support/pallas_call | solution.py:96
  39.2 19.5 %gradient.3 = (f32[40,64,128]{2,1,0:T(8,128)}, bf16[40,64,128]{2,1,0:T(8,128)(2,1)}, bf16[5,64,128]{2,1,0:T(8,128)(2,1)}) custom-call(s32[16]{0:T(128)} %order.9, s32[16]{0:T(128)} %counts.9, s32[1]{0:T(128)} %bitcast.own, bf16[40,512,128]{2,1,0:T(8,128)(2,1)} %collect_support.2.blocks, bf16[40,512,128]{2,1,0:T(8,128)(2,1)} %collect_support.3.blocks_b, ...), custom_call_target="tpu_custom_call" | custom-call | flops 1342177280 | bytes 10485760 | tf_op jit(solution)/shard_map/gradient/pallas_call | solution.py:284
  61.1 1.5 convert_add_fusion.2
  62.7 1.6 collective-permute-start.3
  64.3 8.2 %collective-permute-done.3 = bf16[20,64,128]{2,1,0:T(8,128)(2,1)S(1)} collective-permute-done((bf16[20,64,128]{2,1,0:T(8,128)(2,1)S(1)}, bf16[20,64,128]{2,1,0:T(8,128)(2,1)S(1)}, u32[]{:S(2)}, u32[]{:S(2)}) %collective-permute-start.3) | collective-permute-done | bytes 327712 | tf_op jit(solution)/shard_map/ppermute | solution.py:316
  73.3 3.6 %all-to-all-start.1 = ((bf16[20,64,128]{2,1,0:T(8,128)(2,1)}), bf16[20,64,128]{2,1,0:T(8,128)(2,1)S(1)}, u32[]{:S(2)}, u32[]{:S(2)}) async-start(bf16[20,64,128]{2,1,0:T(8,128)(2,1)} %fusion.2), calls=%async_computation.1 | async-start | bytes 655360 | tf_op jit(solution)/shard_map/all_to_all | solution.py:322
  78.5 8.4 %all-to-all-done.1 = bf16[20,64,128]{2,1,0:T(8,128)(2,1)S(1)} async-done(((bf16[20,64,128]{2,1,0:T(8,128)(2,1)}), bf16[20,64,128]{2,1,0:T(8,128)(2,1)S(1)}, u32[]{:S(2)}, u32[]{:S(2)}) %all-to-all-start.1) | async-done | bytes 327712 | tf_op jit(solution)/shard_map/all_to_all | solution.py:322
  87.1 11.8 %all_to_all.30 = bf16[20,64,128]{2,1,0:T(8,128)(2,1)S(1)} all-to-all(bf16[20,64,128]{2,1,0:T(8,128)(2,1)S(1)} %pad_maximum_fusion.2), channel_id=1, replica_groups={{0,4,8,12},{1,5,9,13},{2,6,10,14},{3,7,11,15},{16,20,24,28},{17,21,25,2..., dimensions={0} | all-to-all | bytes 655360 | tf_op jit(solution)/shard_map/all_to_all | solution.py:322
  98.9 1.5 collective-permute-start.4
  100.5 6.1 %collective-permute-done.4 = bf16[20,64,128]{2,1,0:T(8,128)(2,1)S(1)} collective-permute-done((bf16[20,64,128]{2,1,0:T(8,128)(2,1)S(1)}, bf16[20,64,128]{2,1,0:T(8,128)(2,1)S(1)}, u32[]{:S(2)}, u32[]{:S(2)}) %collective-permute-start.4) | collective-permute-done | bytes 327712 | tf_op jit(solution)/shard_map/ppermute | solution.py:316
  106.7 2.1 collective-permute-done.5.far
  109.7 18.7 %gradient.4 = (f32[40,64,128]{2,1,0:T(8,128)}, bf16[40,64,128]{2,1,0:T(8,128)(2,1)}, bf16[5,64,128]{2,1,0:T(8,128)(2,1)}) custom-call(s32[16]{0:T(128)} %order.9, s32[16]{0:T(128)} %counts.9, s32[1]{0:T(128)} %bitcast.own, bf16[40,512,128]{2,1,0:T(8,128)(2,1)} %collect_support.2.blocks, bf16[40,512,128]{2,1,0:T(8,128)(2,1)} %collect_support.3.blocks_b, ...), custom_call_target="tpu_custom_call" | custom-call | flops 1342177280 | bytes 10485760 | tf_op jit(solution)/shard_map/gradient/pallas_call | solution.py:284
  128.6 2.2 collective-permute-done.6
  130.8 1.5 convert_add_fusion.1
  132.3 1.6 collective-permute-start.7
  133.9 8.2 %collective-permute-done.7 = bf16[20,64,128]{2,1,0:T(8,128)(2,1)S(1)} collective-permute-done((bf16[20,64,128]{2,1,0:T(8,128)(2,1)S(1)}, bf16[20,64,128]{2,1,0:T(8,128)(2,1)S(1)}, u32[]{:S(2)}, u32[]{:S(2)}) %collective-permute-start.7) | collective-permute-done | bytes 327712 | tf_op jit(solution)/shard_map/ppermute | solution.py:316
  142.2 13.2 %all_to_all.31 = bf16[20,64,128]{2,1,0:T(8,128)(2,1)S(1)} all-to-all(bf16[20,64,128]{2,1,0:T(8,128)(2,1)S(1)} %fusion.1), channel_id=1, replica_groups={{0,4,8,12},{1,5,9,13},{2,6,10,14},{3,7,11,15},{16,20,24,28},{17,21,25,2..., dimensions={0} | all-to-all | bytes 655360 | tf_op jit(solution)/shard_map/all_to_all | solution.py:322
  155.6 12.1 %all_to_all.32 = bf16[20,64,128]{2,1,0:T(8,128)(2,1)S(1)} all-to-all(bf16[20,64,128]{2,1,0:T(8,128)(2,1)S(1)} %pad_maximum_fusion.3), channel_id=1, replica_groups={{0,4,8,12},{1,5,9,13},{2,6,10,14},{3,7,11,15},{16,20,24,28},{17,21,25,2..., dimensions={0} | all-to-all | bytes 655360 | tf_op jit(solution)/shard_map/all_to_all | solution.py:322
  167.7 1.5 collective-permute-start.8
  169.2 6.2 %collective-permute-done.8 = bf16[20,64,128]{2,1,0:T(8,128)(2,1)S(1)} collective-permute-done((bf16[20,64,128]{2,1,0:T(8,128)(2,1)S(1)}, bf16[20,64,128]{2,1,0:T(8,128)(2,1)S(1)}, u32[]{:S(2)}, u32[]{:S(2)}) %collective-permute-start.8) | collective-permute-done | bytes 327712 | tf_op jit(solution)/shard_map/ppermute | solution.py:316
  175.5 2.1 collective-permute-done.9.far
  178.4 19.8 %gradient.5 = (f32[64,64,128]{2,1,0:T(8,128)}, bf16[64,64,128]{2,1,0:T(8,128)(2,1)}, bf16[8,64,128]{2,1,0:T(8,128)(2,1)}) custom-call(s32[16]{0:T(128)} %order.9, s32[16]{0:T(128)} %counts.9, s32[1]{0:T(128)} %bitcast.own, bf16[40,512,128]{2,1,0:T(8,128)(2,1)} %collect_support.2.blocks, bf16[40,512,128]{2,1,0:T(8,128)(2,1)} %collect_support.3.blocks_b, ...), custom_call_target="tpu_custom_call" | custom-call | flops 1342177280 | bytes 10485760 | tf_op jit(solution)/shard_map/gradient/pallas_call | solution.py:284
  198.5 2.7 %collective-permute-done.10 = bf16[64,64,128]{2,1,0:T(8,128)(2,1)S(1)} collective-permute-done((bf16[64,64,128]{2,1,0:T(8,128)(2,1)}, bf16[64,64,128]{2,1,0:T(8,128)(2,1)S(1)}, u32[]{:S(2)}, u32[]{:S(2)}) %collective-permute-start.10) | collective-permute-done | bytes 1048608 | tf_op jit(solution)/shard_map/ppermute | solution.py:316
  201.2 1.9 convert_add_fusion
  203.2 1.6 collective-permute-start.11
  204.8 12.4 %collective-permute-done.11 = bf16[32,64,128]{2,1,0:T(8,128)(2,1)S(1)} collective-permute-done((bf16[32,64,128]{2,1,0:T(8,128)(2,1)S(1)}, bf16[32,64,128]{2,1,0:T(8,128)(2,1)S(1)}, u32[]{:S(2)}, u32[]{:S(2)}) %collective-permute-start.11) | collective-permute-done | bytes 524320 | tf_op jit(solution)/shard_map/ppermute | solution.py:316
  218.2 3.8 %all-to-all-start.5 = ((bf16[32,64,128]{2,1,0:T(8,128)(2,1)}), bf16[32,64,128]{2,1,0:T(8,128)(2,1)S(1)}, u32[]{:S(2)}, u32[]{:S(2)}) async-start(bf16[32,64,128]{2,1,0:T(8,128)(2,1)} %fusion), calls=%async_computation.5 | async-start | bytes 1048576 | tf_op jit(solution)/shard_map/all_to_all | solution.py:322
  224.5 11.5 %all-to-all-done.5 = bf16[32,64,128]{2,1,0:T(8,128)(2,1)S(1)} async-done(((bf16[32,64,128]{2,1,0:T(8,128)(2,1)}), bf16[32,64,128]{2,1,0:T(8,128)(2,1)S(1)}, u32[]{:S(2)}, u32[]{:S(2)}) %all-to-all-start.5) | async-done | bytes 524320 | tf_op jit(solution)/shard_map/all_to_all | solution.py:322
  (88 shorter events, 17.2 us)
Async XLA Ops:
  2.5 20.8 %all-to-all-start = ((bf16[32,64,128]{2,1,0:T(8,128)(2,1)}), bf16[32,64,128]{2,1,0:T(8,128)(2,1)S(1)}, u32[]{:S(2)}, u32[]{:S(2)}) async-start(bf16[32,64,128]{2,1,0:T(8,128)(2,1)} %pad_maximum_fusion.1), calls=%async_computation | async-start | bytes 1048576 | tf_op jit(solution)/shard_map/all_to_all | solution.py:322
  23.3 12.9 %collective-permute-start = (bf16[32,64,128]{2,1,0:T(8,128)(2,1)S(1)}, bf16[32,64,128]{2,1,0:T(8,128)(2,1)S(1)}, u32[]{:S(2)}, u32[]{:S(2)}) collective-permute-start(bf16[32,64,128]{2,1,0:T(8,128)(2,1)S(1)} %all-to-all-done), channel_id=1, source_target_pairs={{0,2},{1,3},{2,0},{3,1},{4,6},{5,7},{6,4},{7,5},{8,10},{9,11},{10,... | collective-permute-start | bytes 1572872 | tf_op jit(solution)/shard_map/ppermute | solution.py:316
  35.1 1.2 copy-start.1
  35.2 1.3 copy-start
  35.2 1.9 copy-start.7
  36.3 2.2 copy-start.4
  36.3 2.9 %collective-permute-start.1 = (bf16[64,64,128]{2,1,0:T(8,128)(2,1)S(1)}, bf16[64,64,128]{2,1,0:T(8,128)(2,1)}, u32[]{:S(2)}, u32[]{:S(2)}) collective-permute-start(bf16[64,64,128]{2,1,0:T(8,128)(2,1)S(1)} %pad_maximum_fusion.near), channel_id=1, source_target_pairs={{0,1},{1,0},{2,3},{3,2},{4,5},{5,4},{6,7},{7,6},{8,9},{9,8},{10,11... | collective-permute-start | bytes 3145736 | tf_op jit(solution)/shard_map/ppermute | solution.py:316
  39.2 19.8 %copy-start.2 = (s32[16]{0:T(128)S(1)}, s32[16]{0:T(128)}, u32[]{:S(2)}) copy-start(s32[16]{0:T(128)} %order.9) | copy-start | bytes 196
  58.7 2.4 collective-permute-start.2
  61.1 3.2 %copy-start.12 = (f32[16,64]{1,0:T(8,128)S(1)}, f32[16,64]{1,0:T(8,128)}, u32[]{:S(2)}) copy-start(f32[16,64]{1,0:T(8,128)} %param.13) | copy-start | bytes 12292
  62.7 9.8 %collective-permute-start.3 = (bf16[20,64,128]{2,1,0:T(8,128)(2,1)S(1)}, bf16[20,64,128]{2,1,0:T(8,128)(2,1)S(1)}, u32[]{:S(2)}, u32[]{:S(2)}) collective-permute-start(bf16[20,64,128]{2,1,0:T(8,128)(2,1)S(1)} %slice.53), channel_id=1, source_target_pairs={{0,2},{1,3},{2,0},{3,1},{4,6},{5,7},{6,4},{7,5},{8,10},{9,11},{10,... | collective-permute-start | bytes 983048 | tf_op jit(solution)/shard_map/ppermute | solution.py:316
  73.3 13.7 %copy-start.10 = (bf16[5,64,128]{2,1,0:T(8,128)(2,1)S(1)}, bf16[5,64,128]{2,1,0:T(8,128)(2,1)}, u32[]{:S(2)}) copy-start(bf16[5,64,128]{2,1,0:T(8,128)(2,1)} %get-tuple-element.21) | copy-start | bytes 245764
  73.3 13.6 %all-to-all-start.1 = ((bf16[20,64,128]{2,1,0:T(8,128)(2,1)}), bf16[20,64,128]{2,1,0:T(8,128)(2,1)S(1)}, u32[]{:S(2)}, u32[]{:S(2)}) async-start(bf16[20,64,128]{2,1,0:T(8,128)(2,1)} %fusion.2), calls=%async_computation.1 | async-start | bytes 655360 | tf_op jit(solution)/shard_map/all_to_all | solution.py:322
  98.9 7.7 %collective-permute-start.4 = (bf16[20,64,128]{2,1,0:T(8,128)(2,1)S(1)}, bf16[20,64,128]{2,1,0:T(8,128)(2,1)S(1)}, u32[]{:S(2)}, u32[]{:S(2)}) collective-permute-start(bf16[20,64,128]{2,1,0:T(8,128)(2,1)S(1)} %all_to_all.30), channel_id=1, source_target_pairs={{0,2},{1,3},{2,0},{3,1},{4,6},{5,7},{6,4},{7,5},{8,10},{9,11},{10,... | collective-permute-start | bytes 983048 | tf_op jit(solution)/shard_map/ppermute | solution.py:316
  106.7 2.2 copy-start.5
  106.7 2.2 collective-permute-start.5
  108.8 0.9 copy-start.9
  128.4 2.4 collective-permute-start.6
  132.3 9.8 %collective-permute-start.7 = (bf16[20,64,128]{2,1,0:T(8,128)(2,1)S(1)}, bf16[20,64,128]{2,1,0:T(8,128)(2,1)S(1)}, u32[]{:S(2)}, u32[]{:S(2)}) collective-permute-start(bf16[20,64,128]{2,1,0:T(8,128)(2,1)S(1)} %slice.52), channel_id=1, source_target_pairs={{0,2},{1,3},{2,0},{3,1},{4,6},{5,7},{6,4},{7,5},{8,10},{9,11},{10,... | collective-permute-start | bytes 983048 | tf_op jit(solution)/shard_map/ppermute | solution.py:316
  167.7 7.7 %collective-permute-start.8 = (bf16[20,64,128]{2,1,0:T(8,128)(2,1)S(1)}, bf16[20,64,128]{2,1,0:T(8,128)(2,1)S(1)}, u32[]{:S(2)}, u32[]{:S(2)}) collective-permute-start(bf16[20,64,128]{2,1,0:T(8,128)(2,1)S(1)} %all_to_all.32), channel_id=1, source_target_pairs={{0,2},{1,3},{2,0},{3,1},{4,6},{5,7},{6,4},{7,5},{8,10},{9,11},{10,... | collective-permute-start | bytes 983048 | tf_op jit(solution)/shard_map/ppermute | solution.py:316
  175.4 2.2 copy-start.6
  175.4 2.2 collective-permute-start.9
  177.6 0.8 copy-start.8
  198.3 2.9 %collective-permute-start.10 = (bf16[64,64,128]{2,1,0:T(8,128)(2,1)}, bf16[64,64,128]{2,1,0:T(8,128)(2,1)S(1)}, u32[]{:S(2)}, u32[]{:S(2)}) collective-permute-start(bf16[64,64,128]{2,1,0:T(8,128)(2,1)} %get-tuple-element.28), channel_id=1, source_target_pairs={{0,1},{1,0},{2,3},{3,2},{4,5},{5,4},{6,7},{7,6},{8,9},{9,8},{10,11... | collective-permute-start | bytes 3145736 | tf_op jit(solution)/shard_map/ppermute | solution.py:316
  203.2 18.8 %copy-start.3 = (s32[16]{0:T(128)S(1)}, s32[16]{0:T(128)}, u32[]{:S(2)}) copy-start(s32[16]{0:T(128)} %order.9) | copy-start | bytes 196
  203.2 14.0 %collective-permute-start.11 = (bf16[32,64,128]{2,1,0:T(8,128)(2,1)S(1)}, bf16[32,64,128]{2,1,0:T(8,128)(2,1)S(1)}, u32[]{:S(2)}, u32[]{:S(2)}) collective-permute-start(bf16[32,64,128]{2,1,0:T(8,128)(2,1)S(1)} %slice.51), channel_id=1, source_target_pairs={{0,2},{1,3},{2,0},{3,1},{4,6},{5,7},{6,4},{7,5},{8,10},{9,11},{10,... | collective-permute-start | bytes 1572872 | tf_op jit(solution)/shard_map/ppermute | solution.py:316
  218.2 17.9 %copy-start.11 = (bf16[8,64,128]{2,1,0:T(8,128)(2,1)S(1)}, bf16[8,64,128]{2,1,0:T(8,128)(2,1)}, u32[]{:S(2)}) copy-start(bf16[8,64,128]{2,1,0:T(8,128)(2,1)} %get-tuple-element.26) | copy-start | bytes 393220
  218.2 17.8 %all-to-all-start.5 = ((bf16[32,64,128]{2,1,0:T(8,128)(2,1)}), bf16[32,64,128]{2,1,0:T(8,128)(2,1)S(1)}, u32[]{:S(2)}, u32[]{:S(2)}) async-start(bf16[32,64,128]{2,1,0:T(8,128)(2,1)} %fusion), calls=%async_computation.5 | async-start | bytes 1048576 | tf_op jit(solution)/shard_map/all_to_all | solution.py:322

commit v2 on v0

--- a/solution.py
+++ b/solution.py
@@ -14,8 +14,9 @@
 MEAN_LIVE = 10
 LANES = 2 * BLOCK
 SLOT_PAIRS = SLOTS // 2
-VMEM_LIMIT = 32 * 1024 * 1024
-SUPPORT_VMEM = 58 * 1024 * 1024
+VMEM_LIMIT = 28 * 1024 * 1024
+SUPPORT_VMEM = 34 * 1024 * 1024
+SPARE = SLOT_PAIRS + 2
 
 
 def momentum_list():
@@ -36,9 +37,11 @@
     return lax.broadcasted_iota(jnp.int32, shape, 1) >= BLOCK
 
 
-def support_kernel(begin, order, support, counts, dictionary, out, held, picks, ids, sems, out_sems):
+def support_kernel(begin, order, support, counts, dictionary, *rest):
+    *before, out, held, picks, ids, sems, early_sem = rest
     entries, rows, _ = held.shape
     pairs = entries // 2
+    begin_pair = begin // 2
 
     def fetch(entry, block):
         start = pl.multiple_of((block // 2) * LANES, LANES)
@@ -58,6 +61,9 @@
         return offset + live
 
     lax.fori_loop(0, order.shape[0], start_group, jnp.int32(-begin))
+    early = [pltpu.make_async_copy(ref, out.at[pl.ds(0, begin_pair)], early_sem) for ref in before]
+    for copy in early:
+        copy.start()
     shape = (2 * LANES, LANES)
     source = lax.broadcasted_iota(jnp.int32, shape, 0)
     target = lax.broadcasted_iota(jnp.int32, shape, 1)
@@ -65,57 +71,51 @@
         wanted = jnp.where(target < BLOCK, (choice % 2) * BLOCK + target, LANES + (choice // 2) * BLOCK + target - BLOCK)
         picks[choice] = (source == wanted).astype(jnp.float32).astype(jnp.bfloat16)
 
-    def store(pair):
-        return pltpu.make_async_copy(held.at[2 * pair], out.at[pair], out_sems.at[pair])
-
     def pack(step, carry):
         for pair in (2 * step, 2 * step + 1):
             fetch(2 * pair, ids[2 * pair]).wait()
             fetch(2 * pair + 1, ids[2 * pair + 1]).wait()
-        packed = []
         for pair in (2 * step, 2 * step + 1):
             choice = ids[2 * pair] % 2 + 2 * (ids[2 * pair + 1] % 2)
             both = jnp.concatenate([held[2 * pair], held[2 * pair + 1]], axis=1)
-            packed.append(jnp.dot(both, picks[choice], preferred_element_type=jnp.float32).astype(jnp.bfloat16))
-        for pair, value in zip((2 * step, 2 * step + 1), packed):
-            held[2 * pair] = value
-            store(pair).start()
+            value = jnp.dot(both, picks[choice], preferred_element_type=jnp.float32)
+            out[begin_pair + pair] = value.astype(out.dtype)
         return carry
 
     lax.fori_loop(0, pairs // 2, pack, 0)
-
-    def drain(pair, carry):
-        store(pair).wait()
-        return carry
-
-    lax.fori_loop(0, pairs, drain, 0)
-
-
-def collect_support(order, support, counts, dictionary, begin, entries):
+    rest_pairs = out.shape[0] - begin_pair - pairs
+    if rest_pairs:
+        out[begin_pair + pairs :] = jnp.zeros((rest_pairs,) + out.shape[1:], out.dtype)
+    for copy in early:
+        copy.wait()
+
+
+def collect_support(order, support, counts, dictionary, begin, entries, before=()):
     rows = dictionary.shape[0]
     pairs = entries // 2
+    places = begin // 2 + pairs + SPARE if before else pairs
     return pl.pallas_call(
         functools.partial(support_kernel, begin),
         grid_spec=pltpu.PrefetchScalarGridSpec(
             num_scalar_prefetch=3,
             grid=(),
-            in_specs=[pl.BlockSpec(memory_space=pl.ANY)],
-            out_specs=pl.BlockSpec(memory_space=pl.ANY),
+            in_specs=[pl.BlockSpec(memory_space=pl.ANY)] + [pl.BlockSpec(memory_space=pltpu.VMEM)] * len(before),
+            out_specs=pl.BlockSpec(memory_space=pltpu.VMEM),
             scratch_shapes=[
                 pltpu.VMEM((entries, rows, LANES), dictionary.dtype),
                 pltpu.VMEM((4, 2 * LANES, LANES), jnp.bfloat16),
                 pltpu.SMEM((entries,), jnp.int32),
                 pltpu.SemaphoreType.DMA((entries,)),
-                pltpu.SemaphoreType.DMA((pairs,)),
+                pltpu.SemaphoreType.DMA,
             ],
         ),
-        out_shape=jax.ShapeDtypeStruct((pairs, rows, LANES), dictionary.dtype),
+        out_shape=jax.ShapeDtypeStruct((places, rows, LANES), dictionary.dtype),
         compiler_params=pltpu.CompilerParams(vmem_limit_bytes=SUPPORT_VMEM),
         cost_estimate=pl.CostEstimate(
             flops=0, transcendentals=0, bytes_accessed=3 * pairs * rows * LANES * 2
         ),
         name="collect_support",
-    )(order, support, counts, dictionary)
+    )(order, support, counts, dictionary, *before)
 
 
 def relative_slot(index, me, devices):
@@ -124,34 +124,18 @@
 
 
 def gradient_kernel(
-    packed_in, packed_out, shards, order, counts, own, blocks, blocks_b, near, far, targets, keep, send, extra,
-    held, codes, total, start_codes, offsets, sems, code_sems,
+    packed_in, packed_out, shards, order, counts, own, held, near, far, targets, keep, send, extra,
+    codes, total, start_codes, offsets,
 ):
     groups = order.shape[0]
     me = own[0]
-    pairs = 2 * blocks.shape[0]
-    piece = pairs // shards
+    pairs = held.shape[0] - SPARE
     half_in = near.shape[0]
     shard_in = 2 * half_in // shards
     half_out = keep.shape[0]
     shard_out = 2 * half_out // shards
-
-    def load(index, source=blocks, begin=0):
-        span = pl.ds(index * piece, piece)
-        return pltpu.make_async_copy(source.at[pl.ds(begin, piece)], held.at[span], sems.at[index])
-
-    code_loads = [
-        pltpu.make_async_copy(near, codes.at[pl.ds(0, half_in)], code_sems.at[0]),
-        pltpu.make_async_copy(far, codes.at[pl.ds(half_in, half_in)], code_sems.at[1]),
-    ]
-    for copy in code_loads:
-        copy.start()
-    for index in range(shards):
-        source = (blocks, blocks_b)[2 * index // shards]
-        load(index, source, (index % (shards // 2)) * piece).start()
-    held[pairs:] = jnp.zeros((held.shape[0] - pairs,) + held.shape[1:], held.dtype)
-    for copy in code_loads:
-        copy.wait()
+    codes[:half_in] = near[...]
+    codes[half_in:] = far[...]
 
     upper = upper_half((PATCHES, LANES))
     side = upper.astype(jnp.int32)
@@ -226,8 +210,7 @@
                     value = jnp.zeros((PATCHES, LANES), jnp.float32)
                 total[base + pair] = value
 
-    def two_groups(step, carry):
-        offset, waited = carry
+    def two_groups(step, offset):
         picks = []
         chunks = 1
         for index in (2 * step, 2 * step + 1):
@@ -236,14 +219,6 @@
             picks.append((index, offset, live))
             chunks = jnp.maximum(chunks, (live + offset % 2 + 3) // 4)
             offset = offset + live
-        reach = jnp.minimum(picks[1][1] // 2 + 2 * chunks - 1, pairs - 1)
-        needed = reach // piece + 1
-
-        def wait_piece(index, inner):
-            load(index).wait()
-            return inner
-
-        lax.fori_loop(waited, needed, wait_piece, 0)
         for count in range(1, SLOTS // 4 + 2):
 
             @pl.when(chunks == count)
@@ -251,15 +226,9 @@
                 for pick in picks:
                     one_group(*pick, 2 * count)
 
-        return offset, jnp.maximum(waited, needed)
-
-    _, waited = lax.fori_loop(0, groups // 2, two_groups, (jnp.int32(0), jnp.int32(0)))
-
-    def wait_rest(index, inner):
-        load(index).wait()
-        return inner
-
-    lax.fori_loop(waited, shards, wait_rest, 0)
+        return offset
+
+    lax.fori_loop(0, groups // 2, two_groups, jnp.int32(0))
     keep[...] = total[:half_out]
     send[...] = total[half_out : 2 * half_out].astype(send.dtype)
     if packed_out and not packed_in:
@@ -274,29 +243,25 @@
 
 
 def gradient_call(order, counts, own, blocks, near, far, targets, packed_in, packed_out, shards):
-    pairs, rows, _ = blocks[0].shape
-    pairs = 2 * pairs
+    places, rows, _ = blocks.shape
+    pairs = places - SPARE
     groups = order.shape[0]
     half_in = near.shape[0]
     half_out = (pairs if packed_out else groups * SLOT_PAIRS) // 2
     extra = pairs // shards if packed_out else SLOT_PAIRS
-    spare = SLOT_PAIRS + 2
     tile = (PATCHES, LANES)
     return pl.pallas_call(
         functools.partial(gradient_kernel, packed_in, packed_out, shards),
         grid_spec=pltpu.PrefetchScalarGridSpec(
             num_scalar_prefetch=3,
             grid=(),
-            in_specs=[pl.BlockSpec(memory_space=pl.ANY)] * 4 + [pl.BlockSpec(memory_space=pltpu.VMEM)],
+            in_specs=[pl.BlockSpec(memory_space=pltpu.VMEM)] * 4,
             out_specs=[pl.BlockSpec(memory_space=pltpu.VMEM)] * 3,
             scratch_shapes=[
-                pltpu.VMEM((pairs + spare, rows, LANES), jnp.bfloat16),
                 pltpu.VMEM((2 * half_in,) + tile, jnp.bfloat16),
-                pltpu.VMEM((2 * half_out + spare,) + tile, jnp.float32),
-                pltpu.VMEM((pairs + spare,) + tile, jnp.bfloat16),
+                pltpu.VMEM((2 * half_out + SPARE,) + tile, jnp.float32),
+                pltpu.VMEM((pairs + SPARE,) + tile, jnp.bfloat16),
                 pltpu.SMEM((groups,), jnp.int32),
-                pltpu.SemaphoreType.DMA((shards,)),
-                pltpu.SemaphoreType.DMA((2,)),
             ],
         ),
         out_shape=[
@@ -309,7 +274,7 @@
             flops=4 * pairs * rows * LANES * PATCHES, transcendentals=0, bytes_accessed=pairs * rows * LANES * 2
         ),
         name="gradient",
-    )(order, counts, own, *blocks, near, far, targets)
+    )(order, counts, own, blocks, near, far, targets)
 
 
 def exchange(value, distance):
@@ -317,16 +282,16 @@
     return lax.ppermute(value, "rows", [(i, i ^ distance) for i in range(devices)])
 
 
-def gather_shards(own, beside=()):
+def gather_shards(own, beside=None, finish=None):
     devices = lax.axis_size("rows")
     parts = [own] + [exchange(own, 4 * k) for k in range(1, devices // 4)]
     quarter = jnp.concatenate(parts, axis=0)
-    if beside:
-        quarter, first = lax.optimization_barrier((quarter, beside[0]))
+    if finish is not None:
+        quarter, beside = lax.optimization_barrier((quarter, beside))
     near = jnp.concatenate([quarter, exchange(quarter, 2)], axis=0)
-    if beside:
-        near, second = lax.optimization_barrier((near, beside[1]))
-        return near, exchange(near, 1), (first, second)
+    if finish is not None:
+        near, beside = lax.optimization_barrier((near, finish(beside)))
+        return near, exchange(near, 1), beside
     return near, exchange(near, 1)
 
 
@@ -357,8 +322,10 @@
     pairs = owned_pairs * devices
 
     laid = initial_codes.reshape(SLOT_PAIRS, 2, PATCHES, BLOCK).transpose(0, 2, 1, 3)
-    blocks = [collect_support(group_order, support, counts, dictionary, begin, pairs) for begin in (0, pairs)]
-    near, far, blocks = gather_shards(laid.reshape(SLOT_PAIRS, PATCHES, LANES), blocks)
+    collect = functools.partial(collect_support, group_order, support, counts, dictionary)
+    near, far, blocks = gather_shards(
+        laid.reshape(SLOT_PAIRS, PATCHES, LANES), collect(0, pairs), lambda first: collect(pairs, pairs, (first,))
+    )
 
     own = position.astype(jnp.int32).reshape(1)
     targets = patches.T

time: 218 us -> 206 us (0.945); the launches traced: 219 us -> 204 us
  Pallas kernels: 69.2 us -> 52.7 us
  local copies, waits for them, and re-layouts: 21.4 us -> 24.7 us
    pallas_call x3, Pallas kernels: 48.6 us -> 34.1 us  [gradient_call(): pl.pallas_call(functools.partial(gradient_kernel, packed_in, packed_out,...]
    unnamed x27, local copies, waits for them, and re-layouts: 14.8 us -> 18 us
  transfers between devices with their start and end apart: 30 -> 30, of which waited for: 24 -> 18; matrix products, arithmetic and copies ran while one was open for 3% -> 3% of each run, Pallas kernels for 9% -> 9%
where the time goes in v2:
time: 206 us; the launch traced here: 204 us
  waiting for transfers between devices  85.5 us (42%)
  Pallas kernels  52.7 us (26%)
  starting transfers between devices  35.6 us (17%)
  local copies, waits for them, and re-layouts  24.7 us (12%)
  other arithmetic  3.46 us (2%)
  between operations  2.38 us (1%)
    ppermute x30, waiting for transfers between devices, exchange(): lax.ppermute(value, 'rows', [(i, i ^ distance) for i in range(devices)])  85.5 us
    ppermute x30, starting transfers between devices, exchange(): lax.ppermute(value, 'rows', [(i, i ^ distance) for i in range(devices)])  35.6 us
    pallas_call x3, Pallas kernels, gradient_call(): pl.pallas_call(functools.partial(gradient_kernel, packed_in, packed_out,...  34.1 us
    pallas_call x2, Pallas kernels, collect_support(): pl.pallas_call(functools.partial(support_kernel, begin), grid_spec=pltpu....  18.6 us
    unnamed x27, local copies, waits for them, and re-layouts  18 us
  transfers between devices with their start and end apart: 30, of which 18 were waited for; matrix products, arithmetic and copies ran while one was open for 3% of the time, Pallas kernels for 9%

profile of v2, /device:TPU:0, one launch (start us, length us, event | category | flops | bytes accessed | tf_op | source)
XLA Modules:
  0.0 204.3 jit_solution(13367308457620663111)
XLA Ops:
  1.7 3.1 %collective-permute-start = (bf16[8,64,128]{2,1,0:T(8,128)(2,1)S(1)}, bf16[8,64,128]{2,1,0:T(8,128)(2,1)S(1)}, u32[]{:S(2)}, u32[]{:S(2)}) collective-permute-start(bf16[8,64,128]{2,1,0:T(8,128)(2,1)S(1)} %reshape.124), channel_id=1, source_target_pairs={{0,4},{1,5},{2,6},{3,7},{4,0},{5,1},{6,2},{7,3},{8,12},{9,13},{10,... | collective-permute-start | bytes 393224 | tf_op jit(solution)/shard_map/ppermute | solution.py:282
  4.8 2.6 %collective-permute-start.1 = (bf16[8,64,128]{2,1,0:T(8,128)(2,1)S(1)}, bf16[8,64,128]{2,1,0:T(8,128)(2,1)S(1)}, u32[]{:S(2)}, u32[]{:S(2)}) collective-permute-start(bf16[8,64,128]{2,1,0:T(8,128)(2,1)S(1)} %reshape.124), channel_id=1, source_target_pairs={{0,8},{1,9},{2,10},{3,11},{4,12},{5,13},{6,14},{7,15},{8,0},{9,1},... | collective-permute-start | bytes 393224 | tf_op jit(solution)/shard_map/ppermute | solution.py:282
  7.4 9.0 %collect_support.2.rest_0_ = bf16[40,512,128]{2,1,0:T(8,128)(2,1)S(1)} custom-call(s32[16]{0:T(128)S(1)} %copy-done.1, s32[16,16]{1,0:T(8,128)S(1)} %copy-done.7, s32[16]{0:T(128)S(1)} %copy-done, bf16[512,32768]{1,0:T(8,128)(2,1)} %dictionary.3), custom_call_target="tpu_custom_call" | custom-call | bytes 15728640 | tf_op jit(solution)/shard_map/collect_support/pallas_call | solution.py:97
  17.8 1.6 collective-permute-start.3
  19.3 9.6 %collect_support.3.held = bf16[90,512,128]{2,1,0:T(8,128)(2,1)S(1)} custom-call(s32[16]{0:T(128)S(1)} %copy-done.1, s32[16,16]{1,0:T(8,128)S(1)} %copy-done.7, s32[16]{0:T(128)S(1)} %copy-done, bf16[512,32768]{1,0:T(8,128)(2,1)} %dictionary.3, bf16[40,512,128]{2,1,0:T(8,128)(2,1)S(1)} %collect_support.2.rest_0_), custom_call_target="tpu_custom_call" | custom-call | bytes 15728640 | tf_op jit(solution)/shard_map/collect_support/pallas_call | solution.py:97
  28.9 4.3 %copy-done.2 = bf16[90,512,128]{2,1,0:T(8,128)(2,1)} copy-done((bf16[90,512,128]{2,1,0:T(8,128)(2,1)}, bf16[90,512,128]{2,1,0:T(8,128)(2,1)S(1)}, u32[]{:S(2)}) %copy-start.2) | copy-done | bytes 11796504
  37.1 4.3 %copy-done.3 = bf16[90,512,128]{2,1,0:T(8,128)(2,1)S(1)} copy-done((bf16[90,512,128]{2,1,0:T(8,128)(2,1)S(1)}, bf16[90,512,128]{2,1,0:T(8,128)(2,1)}, u32[]{:S(2)}) %copy-start.3) | copy-done | bytes 11796504
  42.7 11.7 %gradient.3 = (f32[40,64,128]{2,1,0:T(8,128)S(1)}, bf16[40,64,128]{2,1,0:T(8,128)(2,1)}, bf16[5,64,128]{2,1,0:T(8,128)(2,1)S(1)}) custom-call(s32[16]{0:T(128)S(1)} %copy-done.1, s32[16]{0:T(128)S(1)} %copy-done, s32[1]{0:T(128)} %bitcast.own, bf16[90,512,128]{2,1,0:T(8,128)(2,1)S(1)} %copy-done.3, bf16[64,64,128]{2,1,0:T(8,128)(2,1)S(1)} %pad_maximum_fusion.near, ...), custom_call_target="tpu_custom_call" | custom-call | flops 1342177280 | bytes 10485760 | tf_op jit(solution)/shard_map/gradient/pallas_call | solution.py:253
  59.4 8.9 %collective-permute-done.6 = bf16[20,64,128]{2,1,0:T(8,128)(2,1)S(1)} collective-permute-done((bf16[20,64,128]{2,1,0:T(8,128)(2,1)S(1)}, bf16[20,64,128]{2,1,0:T(8,128)(2,1)S(1)}, u32[]{:S(2)}, u32[]{:S(2)}) %collective-permute-start.6) | collective-permute-done | bytes 327712 | tf_op jit(solution)/shard_map/ppermute | solution.py:282
  69.5 2.0 collective-permute-start.7
  74.8 5.6 %collective-permute-done.8 = bf16[5,64,128]{2,1,0:T(8,128)(2,1)S(1)} collective-permute-done((bf16[5,64,128]{2,1,0:T(8,128)(2,1)S(1)}, bf16[5,64,128]{2,1,0:T(8,128)(2,1)S(1)}, u32[]{:S(2)}, u32[]{:S(2)}) %collective-permute-start.8) | collective-permute-done | bytes 81952 | tf_op jit(solution)/shard_map/ppermute | solution.py:282
  83.4 1.6 collective-permute-start.12
  85.9 4.4 %collective-permute-done.11 = bf16[5,64,128]{2,1,0:T(8,128)(2,1)S(1)} collective-permute-done((bf16[5,64,128]{2,1,0:T(8,128)(2,1)S(1)}, bf16[5,64,128]{2,1,0:T(8,128)(2,1)S(1)}, u32[]{:S(2)}, u32[]{:S(2)}) %collective-permute-start.11) | collective-permute-done | bytes 81952 | tf_op jit(solution)/shard_map/ppermute | solution.py:282
  91.0 6.6 %collective-permute-done.13 = bf16[20,64,128]{2,1,0:T(8,128)(2,1)S(1)} collective-permute-done((bf16[20,64,128]{2,1,0:T(8,128)(2,1)S(1)}, bf16[20,64,128]{2,1,0:T(8,128)(2,1)S(1)}, u32[]{:S(2)}, u32[]{:S(2)}) %collective-permute-start.13) | collective-permute-done | bytes 327712 | tf_op jit(solution)/shard_map/ppermute | solution.py:282
  97.6 2.1 %collective-permute-done.14.far = bf16[40,64,128]{2,1,0:T(8,128)(2,1)S(1)} collective-permute-done((bf16[40,64,128]{2,1,0:T(8,128)(2,1)S(1)}, bf16[40,64,128]{2,1,0:T(8,128)(2,1)S(1)}, u32[]{:S(2)}, u32[]{:S(2)}) %collective-permute-start.14) | collective-permute-done | bytes 655392 | tf_op jit(solution)/shard_map/ppermute | solution.py:282
  99.7 4.3 %copy-done.4 = bf16[90,512,128]{2,1,0:T(8,128)(2,1)S(1)} copy-done((bf16[90,512,128]{2,1,0:T(8,128)(2,1)S(1)}, bf16[90,512,128]{2,1,0:T(8,128)(2,1)}, u32[]{:S(2)}) %copy-start.4) | copy-done | bytes 11796504
  104.1 11.1 %gradient.4 = (f32[40,64,128]{2,1,0:T(8,128)S(1)}, bf16[40,64,128]{2,1,0:T(8,128)(2,1)S(1)}, bf16[5,64,128]{2,1,0:T(8,128)(2,1)}) custom-call(s32[16]{0:T(128)S(1)} %copy-done.1, s32[16]{0:T(128)S(1)} %copy-done, s32[1]{0:T(128)} %bitcast.own, bf16[90,512,128]{2,1,0:T(8,128)(2,1)S(1)} %copy-done.4, ...), custom_call_target="tpu_custom_call" | custom-call | flops 1342177280 | bytes 10485760 | tf_op jit(solution)/shard_map/gradient/pallas_call | solution.py:253
  115.3 2.0 collective-permute-done.15
  118.0 9.2 %collective-permute-done.16 = bf16[20,64,128]{2,1,0:T(8,128)(2,1)S(1)} collective-permute-done((bf16[20,64,128]{2,1,0:T(8,128)(2,1)S(1)}, bf16[20,64,128]{2,1,0:T(8,128)(2,1)S(1)}, u32[]{:S(2)}, u32[]{:S(2)}) %collective-permute-start.16) | collective-permute-done | bytes 327712 | tf_op jit(solution)/shard_map/ppermute | solution.py:282
  127.5 2.5 %collective-permute-start.17 = (bf16[5,64,128]{2,1,0:T(8,128)(2,1)S(1)}, bf16[5,64,128]{2,1,0:T(8,128)(2,1)S(1)}, u32[]{:S(2)}, u32[]{:S(2)}) collective-permute-start(bf16[5,64,128]{2,1,0:T(8,128)(2,1)S(1)} %get-tuple-element.44), channel_id=1, source_target_pairs={{0,4},{1,5},{2,6},{3,7},{4,0},{5,1},{6,2},{7,3},{8,12},{9,13},{10,... | collective-permute-start | bytes 245768 | tf_op jit(solution)/shard_map/ppermute | solution.py:282
  129.9 1.8 collective-permute-start.18
  133.2 6.0 %collective-permute-done.18 = bf16[5,64,128]{2,1,0:T(8,128)(2,1)S(1)} collective-permute-done((bf16[5,64,128]{2,1,0:T(8,128)(2,1)S(1)}, bf16[5,64,128]{2,1,0:T(8,128)(2,1)S(1)}, u32[]{:S(2)}, u32[]{:S(2)}) %collective-permute-start.18) | collective-permute-done | bytes 81952 | tf_op jit(solution)/shard_map/ppermute | solution.py:282
  139.4 1.5 collective-permute-start.20
  140.9 1.5 collective-permute-start.21
  144.8 4.7 %collective-permute-done.21 = bf16[5,64,128]{2,1,0:T(8,128)(2,1)S(1)} collective-permute-done((bf16[5,64,128]{2,1,0:T(8,128)(2,1)S(1)}, bf16[5,64,128]{2,1,0:T(8,128)(2,1)S(1)}, u32[]{:S(2)}, u32[]{:S(2)}) %collective-permute-start.21) | collective-permute-done | bytes 81952 | tf_op jit(solution)/shard_map/ppermute | solution.py:282
  150.2 6.6 %collective-permute-done.23 = bf16[20,64,128]{2,1,0:T(8,128)(2,1)S(1)} collective-permute-done((bf16[20,64,128]{2,1,0:T(8,128)(2,1)S(1)}, bf16[20,64,128]{2,1,0:T(8,128)(2,1)S(1)}, u32[]{:S(2)}, u32[]{:S(2)}) %collective-permute-start.23) | collective-permute-done | bytes 327712 | tf_op jit(solution)/shard_map/ppermute | solution.py:282
  156.9 2.1 %collective-permute-done.24.far = bf16[40,64,128]{2,1,0:T(8,128)(2,1)S(1)} collective-permute-done((bf16[40,64,128]{2,1,0:T(8,128)(2,1)S(1)}, bf16[40,64,128]{2,1,0:T(8,128)(2,1)S(1)}, u32[]{:S(2)}, u32[]{:S(2)}) %collective-permute-start.24) | collective-permute-done | bytes 655392 | tf_op jit(solution)/shard_map/ppermute | solution.py:282
  159.0 11.3 %gradient.5 = (f32[64,64,128]{2,1,0:T(8,128)S(1)}, bf16[64,64,128]{2,1,0:T(8,128)(2,1)S(1)}, bf16[8,64,128]{2,1,0:T(8,128)(2,1)S(1)}) custom-call(s32[16]{0:T(128)S(1)} %copy-done.1, s32[16]{0:T(128)S(1)} %copy-done, s32[1]{0:T(128)} %bitcast.own, bf16[90,512,128]{2,1,0:T(8,128)(2,1)S(1)} %copy-done.4, ...), custom_call_target="tpu_custom_call" | custom-call | flops 1342177280 | bytes 10485760 | tf_op jit(solution)/shard_map/gradient/pallas_call | solution.py:253
  170.5 2.5 %collective-permute-done.25 = bf16[64,64,128]{2,1,0:T(8,128)(2,1)S(1)} collective-permute-done((bf16[64,64,128]{2,1,0:T(8,128)(2,1)S(1)}, bf16[64,64,128]{2,1,0:T(8,128)(2,1)S(1)}, u32[]{:S(2)}, u32[]{:S(2)}) %collective-permute-start.25) | collective-permute-done | bytes 1048608 | tf_op jit(solution)/shard_map/ppermute | solution.py:282
  174.1 13.5 %collective-permute-done.26 = bf16[32,64,128]{2,1,0:T(8,128)(2,1)S(1)} collective-permute-done((bf16[32,64,128]{2,1,0:T(8,128)(2,1)S(1)}, bf16[32,64,128]{2,1,0:T(8,128)(2,1)S(1)}, u32[]{:S(2)}, u32[]{:S(2)}) %collective-permute-start.26) | collective-permute-done | bytes 524320 | tf_op jit(solution)/shard_map/ppermute | solution.py:282
  187.8 2.7 %collective-permute-start.27 = (bf16[8,64,128]{2,1,0:T(8,128)(2,1)S(1)}, bf16[8,64,128]{2,1,0:T(8,128)(2,1)S(1)}, u32[]{:S(2)}, u32[]{:S(2)}) collective-permute-start(bf16[8,64,128]{2,1,0:T(8,128)(2,1)S(1)} %get-tuple-element.41), channel_id=1, source_target_pairs={{0,4},{1,5},{2,6},{3,7},{4,0},{5,1},{6,2},{7,3},{8,12},{9,13},{10,... | collective-permute-start | bytes 393224 | tf_op jit(solution)/shard_map/ppermute | solution.py:282
  195.7 7.2 %collective-permute-done.28 = bf16[8,64,128]{2,1,0:T(8,128)(2,1)S(1)} collective-permute-done((bf16[8,64,128]{2,1,0:T(8,128)(2,1)S(1)}, bf16[8,64,128]{2,1,0:T(8,128)(2,1)S(1)}, u32[]{:S(2)}, u32[]{:S(2)}) %collective-permute-start.28) | collective-permute-done | bytes 131104 | tf_op jit(solution)/shard_map/ppermute | solution.py:282
  (113 shorter events, 34.0 us)
Async XLA Ops:
  0.0 7.4 %copy-start.1 = (s32[16]{0:T(128)S(1)}, s32[16]{0:T(128)}, u32[]{:S(2)}) copy-start(s32[16]{0:T(128)} %order.9) | copy-start | bytes 196
  1.7 14.8 %collective-permute-start = (bf16[8,64,128]{2,1,0:T(8,128)(2,1)S(1)}, bf16[8,64,128]{2,1,0:T(8,128)(2,1)S(1)}, u32[]{:S(2)}, u32[]{:S(2)}) collective-permute-start(bf16[8,64,128]{2,1,0:T(8,128)(2,1)S(1)} %reshape.124), channel_id=1, source_target_pairs={{0,4},{1,5},{2,6},{3,7},{4,0},{5,1},{6,2},{7,3},{8,12},{9,13},{10,... | collective-permute-start | bytes 393224 | tf_op jit(solution)/shard_map/ppermute | solution.py:282
  4.8 12.9 %collective-permute-start.1 = (bf16[8,64,128]{2,1,0:T(8,128)(2,1)S(1)}, bf16[8,64,128]{2,1,0:T(8,128)(2,1)S(1)}, u32[]{:S(2)}, u32[]{:S(2)}) collective-permute-start(bf16[8,64,128]{2,1,0:T(8,128)(2,1)S(1)} %reshape.124), channel_id=1, source_target_pairs={{0,8},{1,9},{2,10},{3,11},{4,12},{5,13},{6,14},{7,15},{8,0},{9,1},... | collective-permute-start | bytes 393224 | tf_op jit(solution)/shard_map/ppermute | solution.py:282
  7.3 10.3 %collective-permute-start.2 = (bf16[8,64,128]{2,1,0:T(8,128)(2,1)S(1)}, bf16[8,64,128]{2,1,0:T(8,128)(2,1)S(1)}, u32[]{:S(2)}, u32[]{:S(2)}) collective-permute-start(bf16[8,64,128]{2,1,0:T(8,128)(2,1)S(1)} %reshape.124), channel_id=1, source_target_pairs={{0,12},{1,13},{2,14},{3,15},{4,8},{5,9},{6,10},{7,11},{8,4},{9,5},... | collective-permute-start | bytes 393224 | tf_op jit(solution)/shard_map/ppermute | solution.py:282
  17.8 15.5 %collective-permute-start.3 = (bf16[32,64,128]{2,1,0:T(8,128)(2,1)S(1)}, bf16[32,64,128]{2,1,0:T(8,128)(2,1)S(1)}, u32[]{:S(2)}, u32[]{:S(2)}) collective-permute-start(bf16[32,64,128]{2,1,0:T(8,128)(2,1)S(1)} %pad_maximum_fusion.1), channel_id=1, source_target_pairs={{0,2},{1,3},{2,0},{3,1},{4,6},{5,7},{6,4},{7,5},{8,10},{9,11},{10,... | collective-permute-start | bytes 1572872 | tf_op jit(solution)/shard_map/ppermute | solution.py:282
  33.3 2.7 %collective-permute-start.4 = (bf16[64,64,128]{2,1,0:T(8,128)(2,1)S(1)}, bf16[64,64,128]{2,1,0:T(8,128)(2,1)S(1)}, u32[]{:S(2)}, u32[]{:S(2)}) collective-permute-start(bf16[64,64,128]{2,1,0:T(8,128)(2,1)S(1)} %pad_maximum_fusion.near), channel_id=1, source_target_pairs={{0,1},{1,0},{2,3},{3,2},{4,5},{5,4},{6,7},{7,6},{8,9},{9,8},{10,11... | collective-permute-start | bytes 3145736 | tf_op jit(solution)/shard_map/ppermute | solution.py:282
  42.7 13.0 %copy-start.9 = (f32[16,64]{1,0:T(8,128)S(1)}, f32[16,64]{1,0:T(8,128)}, u32[]{:S(2)}) copy-start(f32[16,64]{1,0:T(8,128)} %param.13) | copy-start | bytes 12292
  54.4 2.4 %collective-permute-start.5 = (bf16[40,64,128]{2,1,0:T(8,128)(2,1)}, bf16[40,64,128]{2,1,0:T(8,128)(2,1)S(1)}, u32[]{:S(2)}, u32[]{:S(2)}) collective-permute-start(bf16[40,64,128]{2,1,0:T(8,128)(2,1)} %get-tuple-element.23), channel_id=1, source_target_pairs={{0,1},{1,0},{2,3},{3,2},{4,5},{5,4},{6,7},{7,6},{8,9},{9,8},{10,11... | collective-permute-start | bytes 1966088 | tf_op jit(solution)/shard_map/ppermute | solution.py:282
  58.2 10.1 %collective-permute-start.6 = (bf16[20,64,128]{2,1,0:T(8,128)(2,1)S(1)}, bf16[20,64,128]{2,1,0:T(8,128)(2,1)S(1)}, u32[]{:S(2)}, u32[]{:S(2)}) collective-permute-start(bf16[20,64,128]{2,1,0:T(8,128)(2,1)S(1)} %slice.144), channel_id=1, source_target_pairs={{0,2},{1,3},{2,0},{3,1},{4,6},{5,7},{6,4},{7,5},{8,10},{9,11},{10,... | collective-permute-start | bytes 983048 | tf_op jit(solution)/shard_map/ppermute | solution.py:282
  69.5 5.3 %collective-permute-start.7 = (bf16[5,64,128]{2,1,0:T(8,128)(2,1)S(1)}, bf16[5,64,128]{2,1,0:T(8,128)(2,1)S(1)}, u32[]{:S(2)}, u32[]{:S(2)}) collective-permute-start(bf16[5,64,128]{2,1,0:T(8,128)(2,1)S(1)} %get-tuple-element.47), channel_id=1, source_target_pairs={{0,4},{1,5},{2,6},{3,7},{4,0},{5,1},{6,2},{7,3},{8,12},{9,13},{10,... | collective-permute-start | bytes 245768 | tf_op jit(solution)/shard_map/ppermute | solution.py:282
  71.5 8.9 %collective-permute-start.8 = (bf16[5,64,128]{2,1,0:T(8,128)(2,1)S(1)}, bf16[5,64,128]{2,1,0:T(8,128)(2,1)S(1)}, u32[]{:S(2)}, u32[]{:S(2)}) collective-permute-start(bf16[5,64,128]{2,1,0:T(8,128)(2,1)S(1)} %get-tuple-element.49), channel_id=1, source_target_pairs={{0,8},{1,9},{2,10},{3,11},{4,12},{5,13},{6,14},{7,15},{8,0},{9,1},... | collective-permute-start | bytes 245768 | tf_op jit(solution)/shard_map/ppermute | solution.py:282
  72.7 7.7 %collective-permute-start.9 = (bf16[5,64,128]{2,1,0:T(8,128)(2,1)S(1)}, bf16[5,64,128]{2,1,0:T(8,128)(2,1)S(1)}, u32[]{:S(2)}, u32[]{:S(2)}) collective-permute-start(bf16[5,64,128]{2,1,0:T(8,128)(2,1)S(1)} %get-tuple-element.48), channel_id=1, source_target_pairs={{0,12},{1,13},{2,14},{3,15},{4,8},{5,9},{6,10},{7,11},{8,4},{9,5},... | collective-permute-start | bytes 245768 | tf_op jit(solution)/shard_map/ppermute | solution.py:282
  80.5 5.3 %collective-permute-start.10 = (bf16[5,64,128]{2,1,0:T(8,128)(2,1)S(1)}, bf16[5,64,128]{2,1,0:T(8,128)(2,1)S(1)}, u32[]{:S(2)}, u32[]{:S(2)}) collective-permute-start(bf16[5,64,128]{2,1,0:T(8,128)(2,1)S(1)} %get-tuple-element.38), channel_id=1, source_target_pairs={{0,4},{1,5},{2,6},{3,7},{4,0},{5,1},{6,2},{7,3},{8,12},{9,13},{10,... | collective-permute-start | bytes 245768 | tf_op jit(solution)/shard_map/ppermute | solution.py:282
  82.0 8.2 %collective-permute-start.11 = (bf16[5,64,128]{2,1,0:T(8,128)(2,1)S(1)}, bf16[5,64,128]{2,1,0:T(8,128)(2,1)S(1)}, u32[]{:S(2)}, u32[]{:S(2)}) collective-permute-start(bf16[5,64,128]{2,1,0:T(8,128)(2,1)S(1)} %get-tuple-element.38), channel_id=1, source_target_pairs={{0,8},{1,9},{2,10},{3,11},{4,12},{5,13},{6,14},{7,15},{8,0},{9,1},... | collective-permute-start | bytes 245768 | tf_op jit(solution)/shard_map/ppermute | solution.py:282
  83.4 6.9 %collective-permute-start.12 = (bf16[5,64,128]{2,1,0:T(8,128)(2,1)S(1)}, bf16[5,64,128]{2,1,0:T(8,128)(2,1)S(1)}, u32[]{:S(2)}, u32[]{:S(2)}) collective-permute-start(bf16[5,64,128]{2,1,0:T(8,128)(2,1)S(1)} %get-tuple-element.38), channel_id=1, source_target_pairs={{0,12},{1,13},{2,14},{3,15},{4,8},{5,9},{6,10},{7,11},{8,4},{9,5},... | collective-permute-start | bytes 245768 | tf_op jit(solution)/shard_map/ppermute | solution.py:282
  90.3 7.2 %collective-permute-start.13 = (bf16[20,64,128]{2,1,0:T(8,128)(2,1)S(1)}, bf16[20,64,128]{2,1,0:T(8,128)(2,1)S(1)}, u32[]{:S(2)}, u32[]{:S(2)}) collective-permute-start(bf16[20,64,128]{2,1,0:T(8,128)(2,1)S(1)} %pad_maximum_fusion.2), channel_id=1, source_target_pairs={{0,2},{1,3},{2,0},{3,1},{4,6},{5,7},{6,4},{7,5},{8,10},{9,11},{10,... | collective-permute-start | bytes 983048 | tf_op jit(solution)/shard_map/ppermute | solution.py:282
  97.6 2.2 %collective-permute-start.14 = (bf16[40,64,128]{2,1,0:T(8,128)(2,1)S(1)}, bf16[40,64,128]{2,1,0:T(8,128)(2,1)S(1)}, u32[]{:S(2)}, u32[]{:S(2)}) collective-permute-start(bf16[40,64,128]{2,1,0:T(8,128)(2,1)S(1)} %constant_dynamic-update-slice_fusion.near), channel_id=1, source_target_pairs={{0,1},{1,0},{2,3},{3,2},{4,5},{5,4},{6,7},{7,6},{8,9},{9,8},{10,11... | collective-permute-start | bytes 1966088 | tf_op jit(solution)/shard_map/ppermute | solution.py:282
  115.1 2.1 %collective-permute-start.15 = (bf16[40,64,128]{2,1,0:T(8,128)(2,1)S(1)}, bf16[40,64,128]{2,1,0:T(8,128)(2,1)S(1)}, u32[]{:S(2)}, u32[]{:S(2)}) collective-permute-start(bf16[40,64,128]{2,1,0:T(8,128)(2,1)S(1)} %get-tuple-element.25), channel_id=1, source_target_pairs={{0,1},{1,0},{2,3},{3,2},{4,5},{5,4},{6,7},{7,6},{8,9},{9,8},{10,11... | collective-permute-start | bytes 1966088 | tf_op jit(solution)/shard_map/ppermute | solution.py:282
  117.5 9.8 %collective-permute-start.16 = (bf16[20,64,128]{2,1,0:T(8,128)(2,1)S(1)}, bf16[20,64,128]{2,1,0:T(8,128)(2,1)S(1)}, u32[]{:S(2)}, u32[]{:S(2)}) collective-permute-start(bf16[20,64,128]{2,1,0:T(8,128)(2,1)S(1)} %slice.143), channel_id=1, source_target_pairs={{0,2},{1,3},{2,0},{3,1},{4,6},{5,7},{6,4},{7,5},{8,10},{9,11},{10,... | collective-permute-start | bytes 983048 | tf_op jit(solution)/shard_map/ppermute | solution.py:282
  127.5 5.7 %collective-permute-start.17 = (bf16[5,64,128]{2,1,0:T(8,128)(2,1)S(1)}, bf16[5,64,128]{2,1,0:T(8,128)(2,1)S(1)}, u32[]{:S(2)}, u32[]{:S(2)}) collective-permute-start(bf16[5,64,128]{2,1,0:T(8,128)(2,1)S(1)} %get-tuple-element.44), channel_id=1, source_target_pairs={{0,4},{1,5},{2,6},{3,7},{4,0},{5,1},{6,2},{7,3},{8,12},{9,13},{10,... | collective-permute-start | bytes 245768 | tf_op jit(solution)/shard_map/ppermute | solution.py:282
  129.9 9.2 %collective-permute-start.18 = (bf16[5,64,128]{2,1,0:T(8,128)(2,1)S(1)}, bf16[5,64,128]{2,1,0:T(8,128)(2,1)S(1)}, u32[]{:S(2)}, u32[]{:S(2)}) collective-permute-start(bf16[5,64,128]{2,1,0:T(8,128)(2,1)S(1)} %get-tuple-element.46), channel_id=1, source_target_pairs={{0,8},{1,9},{2,10},{3,11},{4,12},{5,13},{6,14},{7,15},{8,0},{9,1},... | collective-permute-start | bytes 245768 | tf_op jit(solution)/shard_map/ppermute | solution.py:282
  131.8 7.4 %collective-permute-start.19 = (bf16[5,64,128]{2,1,0:T(8,128)(2,1)S(1)}, bf16[5,64,128]{2,1,0:T(8,128)(2,1)S(1)}, u32[]{:S(2)}, u32[]{:S(2)}) collective-permute-start(bf16[5,64,128]{2,1,0:T(8,128)(2,1)S(1)} %get-tuple-element.45), channel_id=1, source_target_pairs={{0,12},{1,13},{2,14},{3,15},{4,8},{5,9},{6,10},{7,11},{8,4},{9,5},... | collective-permute-start | bytes 245768 | tf_op jit(solution)/shard_map/ppermute | solution.py:282
  139.4 5.4 %collective-permute-start.20 = (bf16[5,64,128]{2,1,0:T(8,128)(2,1)S(1)}, bf16[5,64,128]{2,1,0:T(8,128)(2,1)S(1)}, u32[]{:S(2)}, u32[]{:S(2)}) collective-permute-start(bf16[5,64,128]{2,1,0:T(8,128)(2,1)S(1)} %get-tuple-element.34), channel_id=1, source_target_pairs={{0,4},{1,5},{2,6},{3,7},{4,0},{5,1},{6,2},{7,3},{8,12},{9,13},{10,... | collective-permute-start | bytes 245768 | tf_op jit(solution)/shard_map/ppermute | solution.py:282
  140.9 8.6 %collective-permute-start.21 = (bf16[5,64,128]{2,1,0:T(8,128)(2,1)S(1)}, bf16[5,64,128]{2,1,0:T(8,128)(2,1)S(1)}, u32[]{:S(2)}, u32[]{:S(2)}) collective-permute-start(bf16[5,64,128]{2,1,0:T(8,128)(2,1)S(1)} %get-tuple-element.34), channel_id=1, source_target_pairs={{0,8},{1,9},{2,10},{3,11},{4,12},{5,13},{6,14},{7,15},{8,0},{9,1},... | collective-permute-start | bytes 245768 | tf_op jit(solution)/shard_map/ppermute | solution.py:282
  142.4 7.1 %collective-permute-start.22 = (bf16[5,64,128]{2,1,0:T(8,128)(2,1)S(1)}, bf16[5,64,128]{2,1,0:T(8,128)(2,1)S(1)}, u32[]{:S(2)}, u32[]{:S(2)}) collective-permute-start(bf16[5,64,128]{2,1,0:T(8,128)(2,1)S(1)} %get-tuple-element.34), channel_id=1, source_target_pairs={{0,12},{1,13},{2,14},{3,15},{4,8},{5,9},{6,10},{7,11},{8,4},{9,5},... | collective-permute-start | bytes 245768 | tf_op jit(solution)/shard_map/ppermute | solution.py:282
  149.6 7.2 %collective-permute-start.23 = (bf16[20,64,128]{2,1,0:T(8,128)(2,1)S(1)}, bf16[20,64,128]{2,1,0:T(8,128)(2,1)S(1)}, u32[]{:S(2)}, u32[]{:S(2)}) collective-permute-start(bf16[20,64,128]{2,1,0:T(8,128)(2,1)S(1)} %pad_maximum_fusion.3), channel_id=1, source_target_pairs={{0,2},{1,3},{2,0},{3,1},{4,6},{5,7},{6,4},{7,5},{8,10},{9,11},{10,... | collective-permute-start | bytes 983048 | tf_op jit(solution)/shard_map/ppermute | solution.py:282
  156.8 2.2 %collective-permute-start.24 = (bf16[40,64,128]{2,1,0:T(8,128)(2,1)S(1)}, bf16[40,64,128]{2,1,0:T(8,128)(2,1)S(1)}, u32[]{:S(2)}, u32[]{:S(2)}) collective-permute-start(bf16[40,64,128]{2,1,0:T(8,128)(2,1)S(1)} %constant_dynamic-update-slice_fusion.5.near), channel_id=1, source_target_pairs={{0,1},{1,0},{2,3},{3,2},{4,5},{5,4},{6,7},{7,6},{8,9},{9,8},{10,11... | collective-permute-start | bytes 1966088 | tf_op jit(solution)/shard_map/ppermute | solution.py:282
  170.3 2.7 %collective-permute-start.25 = (bf16[64,64,128]{2,1,0:T(8,128)(2,1)S(1)}, bf16[64,64,128]{2,1,0:T(8,128)(2,1)S(1)}, u32[]{:S(2)}, u32[]{:S(2)}) collective-permute-start(bf16[64,64,128]{2,1,0:T(8,128)(2,1)S(1)} %get-tuple-element.28), channel_id=1, source_target_pairs={{0,1},{1,0},{2,3},{3,2},{4,5},{5,4},{6,7},{7,6},{8,9},{9,8},{10,11... | collective-permute-start | bytes 3145736 | tf_op jit(solution)/shard_map/ppermute | solution.py:282
  173.5 14.0 %collective-permute-start.26 = (bf16[32,64,128]{2,1,0:T(8,128)(2,1)S(1)}, bf16[32,64,128]{2,1,0:T(8,128)(2,1)S(1)}, u32[]{:S(2)}, u32[]{:S(2)}) collective-permute-start(bf16[32,64,128]{2,1,0:T(8,128)(2,1)S(1)} %slice.142), channel_id=1, source_target_pairs={{0,2},{1,3},{2,0},{3,1},{4,6},{5,7},{6,4},{7,5},{8,10},{9,11},{10,... | collective-permute-start | bytes 1572872 | tf_op jit(solution)/shard_map/ppermute | solution.py:282
  187.8 7.9 %collective-permute-start.27 = (bf16[8,64,128]{2,1,0:T(8,128)(2,1)S(1)}, bf16[8,64,128]{2,1,0:T(8,128)(2,1)S(1)}, u32[]{:S(2)}, u32[]{:S(2)}) collective-permute-start(bf16[8,64,128]{2,1,0:T(8,128)(2,1)S(1)} %get-tuple-element.41), channel_id=1, source_target_pairs={{0,4},{1,5},{2,6},{3,7},{4,0},{5,1},{6,2},{7,3},{8,12},{9,13},{10,... | collective-permute-start | bytes 393224 | tf_op jit(solution)/shard_map/ppermute | solution.py:282
  190.5 12.4 %collective-permute-start.28 = (bf16[8,64,128]{2,1,0:T(8,128)(2,1)S(1)}, bf16[8,64,128]{2,1,0:T(8,128)(2,1)S(1)}, u32[]{:S(2)}, u32[]{:S(2)}) collective-permute-start(bf16[8,64,128]{2,1,0:T(8,128)(2,1)S(1)} %get-tuple-element.43), channel_id=1, source_target_pairs={{0,8},{1,9},{2,10},{3,11},{4,12},{5,13},{6,14},{7,15},{8,0},{9,1},... | collective-permute-start | bytes 393224 | tf_op jit(solution)/shard_map/ppermute | solution.py:282
  191.7 11.2 %collective-permute-start.29 = (bf16[8,64,128]{2,1,0:T(8,128)(2,1)S(1)}, bf16[8,64,128]{2,1,0:T(8,128)(2,1)S(1)}, u32[]{:S(2)}, u32[]{:S(2)}) collective-permute-start(bf16[8,64,128]{2,1,0:T(8,128)(2,1)S(1)} %get-tuple-element.42), channel_id=1, source_target_pairs={{0,12},{1,13},{2,14},{3,15},{4,8},{5,9},{6,10},{7,11},{8,4},{9,5},... | collective-permute-start | bytes 393224 | tf_op jit(solution)/shard_map/ppermute | solution.py:282
  (8 other events, 31.1 us)

commit v3 on v2

--- a/solution.py
+++ b/solution.py
@@ -14,8 +14,7 @@
 MEAN_LIVE = 10
 LANES = 2 * BLOCK
 SLOT_PAIRS = SLOTS // 2
-VMEM_LIMIT = 28 * 1024 * 1024
-SUPPORT_VMEM = 34 * 1024 * 1024
+VMEM_MARGIN = 3 * 1024 * 1024
 SPARE = SLOT_PAIRS + 2
 
 
@@ -110,7 +109,7 @@
             ],
         ),
         out_shape=jax.ShapeDtypeStruct((places, rows, LANES), dictionary.dtype),
-        compiler_params=pltpu.CompilerParams(vmem_limit_bytes=SUPPORT_VMEM),
+        compiler_params=pltpu.CompilerParams(vmem_limit_bytes=entries * rows * LANES * 2 + VMEM_MARGIN),
         cost_estimate=pl.CostEstimate(
             flops=0, transcendentals=0, bytes_accessed=3 * pairs * rows * LANES * 2
         ),
@@ -250,6 +249,7 @@
     half_out = (pairs if packed_out else groups * SLOT_PAIRS) // 2
     extra = pairs // shards if packed_out else SLOT_PAIRS
     tile = (PATCHES, LANES)
+    scratch = (2 * half_in * 2 + (2 * half_out + SPARE) * 4 + places * 2) * PATCHES * LANES
     return pl.pallas_call(
         functools.partial(gradient_kernel, packed_in, packed_out, shards),
         grid_spec=pltpu.PrefetchScalarGridSpec(
@@ -260,7 +260,7 @@
             scratch_shapes=[
                 pltpu.VMEM((2 * half_in,) + tile, jnp.bfloat16),
                 pltpu.VMEM((2 * half_out + SPARE,) + tile, jnp.float32),
-                pltpu.VMEM((pairs + SPARE,) + tile, jnp.bfloat16),
+                pltpu.VMEM((places,) + tile, jnp.bfloat16),
                 pltpu.SMEM((groups,), jnp.int32),
             ],
         ),
@@ -269,7 +269,7 @@
             jax.ShapeDtypeStruct((half_out,) + tile, jnp.bfloat16),
             jax.ShapeDtypeStruct((extra,) + tile, jnp.bfloat16),
         ],
-        compiler_params=pltpu.CompilerParams(vmem_limit_bytes=VMEM_LIMIT),
+        compiler_params=pltpu.CompilerParams(vmem_limit_bytes=scratch + VMEM_MARGIN),
         cost_estimate=pl.CostEstimate(
             flops=4 * pairs * rows * LANES * PATCHES, transcendentals=0, bytes_accessed=pairs * rows * LANES * 2
         ),
@@ -282,29 +282,34 @@
     return lax.ppermute(value, "rows", [(i, i ^ distance) for i in range(devices)])
 
 
-def gather_shards(own, beside=None, finish=None):
-    devices = lax.axis_size("rows")
-    parts = [own] + [exchange(own, 4 * k) for k in range(1, devices // 4)]
-    quarter = jnp.concatenate(parts, axis=0)
-    if finish is not None:
-        quarter, beside = lax.optimization_barrier((quarter, beside))
+def distances():
+    columns = lax.axis_size("rows") // 4
+    return [4 * column + 2 * row for row in range(2) for column in range(columns)]
+
+
+def gather_staged(own, beside, finish):
+    columns = lax.axis_size("rows") // 4
+    quarter = jnp.concatenate([own] + [exchange(own, 4 * k) for k in range(1, columns)], axis=0)
+    quarter, beside = lax.optimization_barrier((quarter, beside))
     near = jnp.concatenate([quarter, exchange(quarter, 2)], axis=0)
-    if finish is not None:
-        near, beside = lax.optimization_barrier((near, finish(beside)))
-        return near, exchange(near, 1), beside
+    near, beside = lax.optimization_barrier((near, finish(beside)))
+    return near, exchange(near, 1), beside
+
+
+def gather_shards(own):
+    near = jnp.concatenate([own] + [exchange(own, distance) for distance in distances()[1:]], axis=0)
     return near, exchange(near, 1)
 
 
 def reduce_shards(keep, send):
-    devices = lax.axis_size("rows")
     half = keep + exchange(send, 1).astype(jnp.float32)
-    middle = half.shape[0] // 2
-    quarter = half[:middle] + exchange(half[middle:].astype(jnp.bfloat16), 2).astype(jnp.float32)
-    size = quarter.shape[0] // (devices // 4)
-    sent = quarter.astype(jnp.bfloat16)
-    total = quarter[:size]
-    for k in range(1, devices // 4):
-        total = total + exchange(sent[k * size : (k + 1) * size], 4 * k).astype(jnp.float32)
+    apart = distances()
+    size = half.shape[0] // len(apart)
+    sent = half.astype(jnp.bfloat16)
+    total = half[:size]
+    for place in range(1, len(apart)):
+        share = exchange(sent[place * size : (place + 1) * size], apart[place])
+        total = total + share.astype(jnp.float32)
     return total
 
 
@@ -323,7 +328,7 @@
 
     laid = initial_codes.reshape(SLOT_PAIRS, 2, PATCHES, BLOCK).transpose(0, 2, 1, 3)
     collect = functools.partial(collect_support, group_order, support, counts, dictionary)
-    near, far, blocks = gather_shards(
+    near, far, blocks = gather_staged(
         laid.reshape(SLOT_PAIRS, PATCHES, LANES), collect(0, pairs), lambda first: collect(pairs, pairs, (first,))
     )
 

time: 206 us -> 215 us (1.044)
  waiting for transfers between devices: 85.5 us -> 48.6 us
  starting transfers between devices: 35.6 us -> 65.1 us
  local copies, waits for them, and re-layouts: 24.7 us -> 37.6 us
  Pallas kernels: 52.7 us -> 55.8 us
    ppermute x30 -> x45, waiting for transfers between devices: 85.5 us -> 48.6 us  [exchange(): lax.ppermute(value, 'rows', [(i, i ^ distance) for i in range(devices)])]
    ppermute x30 -> x45, starting transfers between devices: 35.6 us -> 65.1 us  [exchange(): lax.ppermute(value, 'rows', [(i, i ^ distance) for i in range(devices)])]
    unnamed x27 -> x43, local copies, waits for them, and re-layouts: 18 us -> 29.7 us
    pallas_call x2, Pallas kernels: 18.6 us -> 21.7 us  [collect_support(): pl.pallas_call(functools.partial(support_kernel, begin), grid_spec=pltpu....]
  transfers between devices with their start and end apart: 30 -> 45, of which waited for: 18 -> 20; matrix products, arithmetic and copies ran while one was open for 3% -> 2% of each run, Pallas kernels for 9% -> 10%
where the time goes in v3:
time: 215 us; the launch traced here: 213 us
  starting transfers between devices  65.1 us (30%)
  Pallas kernels  55.8 us (26%)
  waiting for transfers between devices  48.6 us (23%)
  local copies, waits for them, and re-layouts  37.6 us (17%)
  other arithmetic  4.13 us (2%)
  between operations  2.2 us (1%)
    ppermute x45, starting transfers between devices, exchange(): lax.ppermute(value, 'rows', [(i, i ^ distance) for i in range(devices)])  65.1 us
    ppermute x45, waiting for transfers between devices, exchange(): lax.ppermute(value, 'rows', [(i, i ^ distance) for i in range(devices)])  48.6 us
    pallas_call x3, Pallas kernels, gradient_call(): pl.pallas_call(functools.partial(gradient_kernel, packed_in, packed_out,...  34.1 us
    unnamed x43, local copies, waits for them, and re-layouts  29.7 us
    pallas_call x2, Pallas kernels, collect_support(): pl.pallas_call(functools.partial(support_kernel, begin), grid_spec=pltpu....  21.7 us
  transfers between devices with their start and end apart: 45, of which 20 were waited for; matrix products, arithmetic and copies ran while one was open for 2% of the time, Pallas kernels for 10%

profile of v3, /device:TPU:0, one launch (start us, length us, event | category | flops | bytes accessed | tf_op | source)
XLA Modules:
  0.0 213.4 jit_solution(3993904939581119053)
XLA Ops:
  1.7 3.1 %collective-permute-start = (bf16[8,64,128]{2,1,0:T(8,128)(2,1)S(1)}, bf16[8,64,128]{2,1,0:T(8,128)(2,1)S(1)}, u32[]{:S(2)}, u32[]{:S(2)}) collective-permute-start(bf16[8,64,128]{2,1,0:T(8,128)(2,1)S(1)} %reshape.124), channel_id=1, source_target_pairs={{0,4},{1,5},{2,6},{3,7},{4,0},{5,1},{6,2},{7,3},{8,12},{9,13},{10,... | collective-permute-start | bytes 393224 | tf_op jit(solution)/shard_map/ppermute | solution.py:282
  4.8 2.6 %collective-permute-start.1 = (bf16[8,64,128]{2,1,0:T(8,128)(2,1)S(1)}, bf16[8,64,128]{2,1,0:T(8,128)(2,1)S(1)}, u32[]{:S(2)}, u32[]{:S(2)}) collective-permute-start(bf16[8,64,128]{2,1,0:T(8,128)(2,1)S(1)} %reshape.124), channel_id=1, source_target_pairs={{0,8},{1,9},{2,10},{3,11},{4,12},{5,13},{6,14},{7,15},{8,0},{9,1},... | collective-permute-start | bytes 393224 | tf_op jit(solution)/shard_map/ppermute | solution.py:282
  7.4 10.5 %copy-done.5 = bf16[512,32768]{1,0:T(8,128)(2,1)S(1)} copy-done((bf16[512,32768]{1,0:T(8,128)(2,1)S(1)}, bf16[512,32768]{1,0:T(8,128)(2,1)}, u32[]{:S(2)}) %copy-start.5) | copy-done | bytes 33554456
  17.9 12.1 %collect_support.2.rest_0_ = bf16[40,512,128]{2,1,0:T(8,128)(2,1)S(1)} custom-call(s32[16]{0:T(128)S(1)} %copy-done.1, s32[16,16]{1,0:T(8,128)S(1)} %copy-done.8, s32[16]{0:T(128)S(1)} %copy-done, bf16[512,32768]{1,0:T(8,128)(2,1)S(1)} %copy-done.5), custom_call_target="tpu_custom_call" | custom-call | bytes 15728640 | tf_op jit(solution)/shard_map/collect_support/pallas_call | solution.py:96
  30.1 2.3 %copy-done.6 = bf16[40,512,128]{2,1,0:T(8,128)(2,1)} copy-done((bf16[40,512,128]{2,1,0:T(8,128)(2,1)}, bf16[40,512,128]{2,1,0:T(8,128)(2,1)S(1)}, u32[]{:S(2)}) %copy-start.6) | copy-done | bytes 5242904
  34.8 2.5 %copy-done.7 = bf16[40,512,128]{2,1,0:T(8,128)(2,1)S(1)} copy-done((bf16[40,512,128]{2,1,0:T(8,128)(2,1)S(1)}, bf16[40,512,128]{2,1,0:T(8,128)(2,1)}, u32[]{:S(2)}) %copy-start.7) | copy-done | bytes 5242904
  37.3 9.6 %collect_support.3.held = bf16[90,512,128]{2,1,0:T(8,128)(2,1)S(1)} custom-call(s32[16]{0:T(128)S(1)} %copy-done.1, s32[16,16]{1,0:T(8,128)S(1)} %copy-done.8, s32[16]{0:T(128)S(1)} %copy-done, bf16[512,32768]{1,0:T(8,128)(2,1)} %dictionary.3, bf16[40,512,128]{2,1,0:T(8,128)(2,1)S(1)} %copy-done.7), custom_call_target="tpu_custom_call" | custom-call | bytes 15728640 | tf_op jit(solution)/shard_map/collect_support/pallas_call | solution.py:96
  46.9 4.3 %copy-done.2 = bf16[90,512,128]{2,1,0:T(8,128)(2,1)} copy-done((bf16[90,512,128]{2,1,0:T(8,128)(2,1)}, bf16[90,512,128]{2,1,0:T(8,128)(2,1)S(1)}, u32[]{:S(2)}) %copy-start.2) | copy-done | bytes 11796504
  54.0 4.3 %copy-done.3 = bf16[90,512,128]{2,1,0:T(8,128)(2,1)S(1)} copy-done((bf16[90,512,128]{2,1,0:T(8,128)(2,1)S(1)}, bf16[90,512,128]{2,1,0:T(8,128)(2,1)}, u32[]{:S(2)}) %copy-start.3) | copy-done | bytes 11796504
  58.3 11.2 %gradient.3 = (f32[40,64,128]{2,1,0:T(8,128)S(1)}, bf16[40,64,128]{2,1,0:T(8,128)(2,1)S(1)}, bf16[5,64,128]{2,1,0:T(8,128)(2,1)S(1)}) custom-call(s32[16]{0:T(128)S(1)} %copy-done.1, s32[16]{0:T(128)S(1)} %copy-done, s32[1]{0:T(128)} %bitcast.own, bf16[90,512,128]{2,1,0:T(8,128)(2,1)S(1)} %copy-done.3, bf16[64,64,128]{2,1,0:T(8,128)(2,1)S(1)} %pad_maximum_fusion.near, ...), custom_call_target="tpu_custom_call" | custom-call | flops 1342177280 | bytes 10485760 | tf_op jit(solution)/shard_map/gradient/pallas_call | solution.py:253
  73.9 3.9 %collective-permute-start.11 = (bf16[5,64,128]{2,1,0:T(8,128)(2,1)S(1)}, bf16[5,64,128]{2,1,0:T(8,128)(2,1)S(1)}, u32[]{:S(2)}, u32[]{:S(2)}) collective-permute-start(bf16[5,64,128]{2,1,0:T(8,128)(2,1)S(1)} %get-tuple-element.58), channel_id=1, source_target_pairs={{0,10},{1,11},{2,8},{3,9},{4,14},{5,15},{6,12},{7,13},{8,2},{9,3},... | collective-permute-start | bytes 245768 | tf_op jit(solution)/shard_map/ppermute | solution.py:282
  79.2 4.2 %collective-permute-start.7 = (bf16[5,64,128]{2,1,0:T(8,128)(2,1)S(1)}, bf16[5,64,128]{2,1,0:T(8,128)(2,1)}, u32[]{:S(2)}, u32[]{:S(2)}) collective-permute-start(bf16[5,64,128]{2,1,0:T(8,128)(2,1)S(1)} %get-tuple-element.62), channel_id=1, source_target_pairs={{0,8},{1,9},{2,10},{3,11},{4,12},{5,13},{6,14},{7,15},{8,0},{9,1},... | collective-permute-start | bytes 245768 | tf_op jit(solution)/shard_map/ppermute | solution.py:282
  86.8 4.2 %collective-permute-done.7 = bf16[5,64,128]{2,1,0:T(8,128)(2,1)} collective-permute-done((bf16[5,64,128]{2,1,0:T(8,128)(2,1)S(1)}, bf16[5,64,128]{2,1,0:T(8,128)(2,1)}, u32[]{:S(2)}, u32[]{:S(2)}) %collective-permute-start.7) | collective-permute-done | bytes 81952 | tf_op jit(solution)/shard_map/ppermute | solution.py:282
  99.0 2.3 %collective-permute-start.18 = (bf16[5,64,128]{2,1,0:T(8,128)(2,1)S(1)}, bf16[5,64,128]{2,1,0:T(8,128)(2,1)S(1)}, u32[]{:S(2)}, u32[]{:S(2)}) collective-permute-start(bf16[5,64,128]{2,1,0:T(8,128)(2,1)S(1)} %get-tuple-element.38), channel_id=1, source_target_pairs={{0,10},{1,11},{2,8},{3,9},{4,14},{5,15},{6,12},{7,13},{8,2},{9,3},... | collective-permute-start | bytes 245768 | tf_op jit(solution)/shard_map/ppermute | solution.py:282
  101.3 2.4 %collective-permute-done.14 = bf16[5,64,128]{2,1,0:T(8,128)(2,1)S(1)} collective-permute-done((bf16[5,64,128]{2,1,0:T(8,128)(2,1)S(1)}, bf16[5,64,128]{2,1,0:T(8,128)(2,1)S(1)}, u32[]{:S(2)}, u32[]{:S(2)}) %collective-permute-start.14) | collective-permute-done | bytes 81952 | tf_op jit(solution)/shard_map/ppermute | solution.py:282
  103.7 2.9 %collective-permute-start.19 = (bf16[5,64,128]{2,1,0:T(8,128)(2,1)S(1)}, bf16[5,64,128]{2,1,0:T(8,128)(2,1)S(1)}, u32[]{:S(2)}, u32[]{:S(2)}) collective-permute-start(bf16[5,64,128]{2,1,0:T(8,128)(2,1)S(1)} %get-tuple-element.38), channel_id=1, source_target_pairs={{0,14},{1,15},{2,12},{3,13},{4,10},{5,11},{6,8},{7,9},{8,6},{9,7},... | collective-permute-start | bytes 245768 | tf_op jit(solution)/shard_map/ppermute | solution.py:282
  106.7 3.1 %collective-permute-done.18 = bf16[5,64,128]{2,1,0:T(8,128)(2,1)S(1)} collective-permute-done((bf16[5,64,128]{2,1,0:T(8,128)(2,1)S(1)}, bf16[5,64,128]{2,1,0:T(8,128)(2,1)S(1)}, u32[]{:S(2)}, u32[]{:S(2)}) %collective-permute-start.18) | collective-permute-done | bytes 81952 | tf_op jit(solution)/shard_map/ppermute | solution.py:282
  111.1 2.1 collective-permute-done.20.far
  113.1 4.3 %copy-done.4 = bf16[90,512,128]{2,1,0:T(8,128)(2,1)S(1)} copy-done((bf16[90,512,128]{2,1,0:T(8,128)(2,1)S(1)}, bf16[90,512,128]{2,1,0:T(8,128)(2,1)}, u32[]{:S(2)}) %copy-start.4) | copy-done | bytes 11796504
  117.5 11.3 %gradient.4 = (f32[40,64,128]{2,1,0:T(8,128)S(1)}, bf16[40,64,128]{2,1,0:T(8,128)(2,1)S(1)}, bf16[5,64,128]{2,1,0:T(8,128)(2,1)}) custom-call(s32[16]{0:T(128)S(1)} %copy-done.1, s32[16]{0:T(128)S(1)} %copy-done, s32[1]{0:T(128)} %bitcast.own, bf16[90,512,128]{2,1,0:T(8,128)(2,1)S(1)} %copy-done.4, ...), custom_call_target="tpu_custom_call" | custom-call | flops 1342177280 | bytes 10485760 | tf_op jit(solution)/shard_map/gradient/pallas_call | solution.py:253
  137.5 3.2 %collective-permute-start.27 = (bf16[5,64,128]{2,1,0:T(8,128)(2,1)S(1)}, bf16[5,64,128]{2,1,0:T(8,128)(2,1)S(1)}, u32[]{:S(2)}, u32[]{:S(2)}) collective-permute-start(bf16[5,64,128]{2,1,0:T(8,128)(2,1)S(1)} %get-tuple-element.51), channel_id=1, source_target_pairs={{0,10},{1,11},{2,8},{3,9},{4,14},{5,15},{6,12},{7,13},{8,2},{9,3},... | collective-permute-start | bytes 245768 | tf_op jit(solution)/shard_map/ppermute | solution.py:282
  142.1 2.5 %collective-permute-start.28 = (bf16[5,64,128]{2,1,0:T(8,128)(2,1)S(1)}, bf16[5,64,128]{2,1,0:T(8,128)(2,1)S(1)}, u32[]{:S(2)}, u32[]{:S(2)}) collective-permute-start(bf16[5,64,128]{2,1,0:T(8,128)(2,1)S(1)} %get-tuple-element.50), channel_id=1, source_target_pairs={{0,14},{1,15},{2,12},{3,13},{4,10},{5,11},{6,8},{7,9},{8,6},{9,7},... | collective-permute-start | bytes 245768 | tf_op jit(solution)/shard_map/ppermute | solution.py:282
  144.6 3.9 %collective-permute-done.27 = bf16[5,64,128]{2,1,0:T(8,128)(2,1)S(1)} collective-permute-done((bf16[5,64,128]{2,1,0:T(8,128)(2,1)S(1)}, bf16[5,64,128]{2,1,0:T(8,128)(2,1)S(1)}, u32[]{:S(2)}, u32[]{:S(2)}) %collective-permute-start.27) | collective-permute-done | bytes 81952 | tf_op jit(solution)/shard_map/ppermute | solution.py:282
  156.0 2.7 %collective-permute-start.34 = (bf16[5,64,128]{2,1,0:T(8,128)(2,1)S(1)}, bf16[5,64,128]{2,1,0:T(8,128)(2,1)S(1)}, u32[]{:S(2)}, u32[]{:S(2)}) collective-permute-start(bf16[5,64,128]{2,1,0:T(8,128)(2,1)S(1)} %get-tuple-element.34), channel_id=1, source_target_pairs={{0,10},{1,11},{2,8},{3,9},{4,14},{5,15},{6,12},{7,13},{8,2},{9,3},... | collective-permute-start | bytes 245768 | tf_op jit(solution)/shard_map/ppermute | solution.py:282
  160.8 2.7 %collective-permute-start.35 = (bf16[5,64,128]{2,1,0:T(8,128)(2,1)S(1)}, bf16[5,64,128]{2,1,0:T(8,128)(2,1)S(1)}, u32[]{:S(2)}, u32[]{:S(2)}) collective-permute-start(bf16[5,64,128]{2,1,0:T(8,128)(2,1)S(1)} %get-tuple-element.34), channel_id=1, source_target_pairs={{0,14},{1,15},{2,12},{3,13},{4,10},{5,11},{6,8},{7,9},{8,6},{9,7},... | collective-permute-start | bytes 245768 | tf_op jit(solution)/shard_map/ppermute | solution.py:282
  163.6 2.8 %collective-permute-done.34 = bf16[5,64,128]{2,1,0:T(8,128)(2,1)S(1)} collective-permute-done((bf16[5,64,128]{2,1,0:T(8,128)(2,1)S(1)}, bf16[5,64,128]{2,1,0:T(8,128)(2,1)S(1)}, u32[]{:S(2)}, u32[]{:S(2)}) %collective-permute-start.34) | collective-permute-done | bytes 81952 | tf_op jit(solution)/shard_map/ppermute | solution.py:282
  168.1 2.1 collective-permute-done.36.far
  170.2 11.5 %gradient.5 = (f32[64,64,128]{2,1,0:T(8,128)S(1)}, bf16[64,64,128]{2,1,0:T(8,128)(2,1)S(1)}, bf16[8,64,128]{2,1,0:T(8,128)(2,1)S(1)}) custom-call(s32[16]{0:T(128)S(1)} %copy-done.1, s32[16]{0:T(128)S(1)} %copy-done, s32[1]{0:T(128)} %bitcast.own, bf16[90,512,128]{2,1,0:T(8,128)(2,1)S(1)} %bitcast.31, ...), custom_call_target="tpu_custom_call" | custom-call | flops 1342177280 | bytes 10485760 | tf_op jit(solution)/shard_map/gradient/pallas_call | solution.py:253
  181.9 2.5 %collective-permute-done.37 = bf16[64,64,128]{2,1,0:T(8,128)(2,1)S(1)} collective-permute-done((bf16[64,64,128]{2,1,0:T(8,128)(2,1)S(1)}, bf16[64,64,128]{2,1,0:T(8,128)(2,1)S(1)}, u32[]{:S(2)}, u32[]{:S(2)}) %collective-permute-start.37) | collective-permute-done | bytes 1048608 | tf_op jit(solution)/shard_map/ppermute | solution.py:282
  194.8 4.5 %collective-permute-done.39 = bf16[8,64,128]{2,1,0:T(8,128)(2,1)S(1)} collective-permute-done((bf16[8,64,128]{2,1,0:T(8,128)(2,1)S(1)}, bf16[8,64,128]{2,1,0:T(8,128)(2,1)S(1)}, u32[]{:S(2)}, u32[]{:S(2)}) %collective-permute-start.39) | collective-permute-done | bytes 131104 | tf_op jit(solution)/shard_map/ppermute | solution.py:282
  199.3 2.8 %collective-permute-start.44 = (bf16[8,64,128]{2,1,0:T(8,128)(2,1)S(1)}, bf16[8,64,128]{2,1,0:T(8,128)(2,1)S(1)}, u32[]{:S(2)}, u32[]{:S(2)}) collective-permute-start(bf16[8,64,128]{2,1,0:T(8,128)(2,1)S(1)} %get-tuple-element.43), channel_id=1, source_target_pairs={{0,14},{1,15},{2,12},{3,13},{4,10},{5,11},{6,8},{7,9},{8,6},{9,7},... | collective-permute-start | bytes 393224 | tf_op jit(solution)/shard_map/ppermute | solution.py:282
  204.5 5.8 %collective-permute-done.43 = bf16[8,64,128]{2,1,0:T(8,128)(2,1)S(1)} collective-permute-done((bf16[8,64,128]{2,1,0:T(8,128)(2,1)S(1)}, bf16[8,64,128]{2,1,0:T(8,128)(2,1)S(1)}, u32[]{:S(2)}, u32[]{:S(2)}) %collective-permute-start.43) | collective-permute-done | bytes 131104 | tf_op jit(solution)/shard_map/ppermute | solution.py:282
  (152 shorter events, 60.9 us)
Async XLA Ops:
  1.7 30.7 %collective-permute-start = (bf16[8,64,128]{2,1,0:T(8,128)(2,1)S(1)}, bf16[8,64,128]{2,1,0:T(8,128)(2,1)S(1)}, u32[]{:S(2)}, u32[]{:S(2)}) collective-permute-start(bf16[8,64,128]{2,1,0:T(8,128)(2,1)S(1)} %reshape.124), channel_id=1, source_target_pairs={{0,4},{1,5},{2,6},{3,7},{4,0},{5,1},{6,2},{7,3},{8,12},{9,13},{10,... | collective-permute-start | bytes 393224 | tf_op jit(solution)/shard_map/ppermute | solution.py:282
  4.8 27.6 %collective-permute-start.1 = (bf16[8,64,128]{2,1,0:T(8,128)(2,1)S(1)}, bf16[8,64,128]{2,1,0:T(8,128)(2,1)S(1)}, u32[]{:S(2)}, u32[]{:S(2)}) collective-permute-start(bf16[8,64,128]{2,1,0:T(8,128)(2,1)S(1)} %reshape.124), channel_id=1, source_target_pairs={{0,8},{1,9},{2,10},{3,11},{4,12},{5,13},{6,14},{7,15},{8,0},{9,1},... | collective-permute-start | bytes 393224 | tf_op jit(solution)/shard_map/ppermute | solution.py:282
  7.3 25.1 %collective-permute-start.2 = (bf16[8,64,128]{2,1,0:T(8,128)(2,1)S(1)}, bf16[8,64,128]{2,1,0:T(8,128)(2,1)S(1)}, u32[]{:S(2)}, u32[]{:S(2)}) collective-permute-start(bf16[8,64,128]{2,1,0:T(8,128)(2,1)S(1)} %reshape.124), channel_id=1, source_target_pairs={{0,12},{1,13},{2,14},{3,15},{4,8},{5,9},{6,10},{7,11},{8,4},{9,5},... | collective-permute-start | bytes 393224 | tf_op jit(solution)/shard_map/ppermute | solution.py:282
  32.5 18.7 %collective-permute-start.3 = (bf16[32,64,128]{2,1,0:T(8,128)(2,1)S(1)}, bf16[32,64,128]{2,1,0:T(8,128)(2,1)S(1)}, u32[]{:S(2)}, u32[]{:S(2)}) collective-permute-start(bf16[32,64,128]{2,1,0:T(8,128)(2,1)S(1)} %pad_maximum_fusion.1), channel_id=1, source_target_pairs={{0,2},{1,3},{2,0},{3,1},{4,6},{5,7},{6,4},{7,5},{8,10},{9,11},{10,... | collective-permute-start | bytes 1572872 | tf_op jit(solution)/shard_map/ppermute | solution.py:282
  72.7 10.6 %collective-permute-start.10 = (bf16[5,64,128]{2,1,0:T(8,128)(2,1)S(1)}, bf16[5,64,128]{2,1,0:T(8,128)(2,1)S(1)}, u32[]{:S(2)}, u32[]{:S(2)}) collective-permute-start(bf16[5,64,128]{2,1,0:T(8,128)(2,1)S(1)} %get-tuple-element.59), channel_id=1, source_target_pairs={{0,6},{1,7},{2,4},{3,5},{4,2},{5,3},{6,0},{7,1},{8,14},{9,15},{10,... | collective-permute-start | bytes 245768 | tf_op jit(solution)/shard_map/ppermute | solution.py:282
  73.9 9.6 %collective-permute-start.11 = (bf16[5,64,128]{2,1,0:T(8,128)(2,1)S(1)}, bf16[5,64,128]{2,1,0:T(8,128)(2,1)S(1)}, u32[]{:S(2)}, u32[]{:S(2)}) collective-permute-start(bf16[5,64,128]{2,1,0:T(8,128)(2,1)S(1)} %get-tuple-element.58), channel_id=1, source_target_pairs={{0,10},{1,11},{2,8},{3,9},{4,14},{5,15},{6,12},{7,13},{8,2},{9,3},... | collective-permute-start | bytes 245768 | tf_op jit(solution)/shard_map/ppermute | solution.py:282
  78.4 8.4 %collective-permute-start.12 = (bf16[5,64,128]{2,1,0:T(8,128)(2,1)}, bf16[5,64,128]{2,1,0:T(8,128)(2,1)S(1)}, u32[]{:S(2)}, u32[]{:S(2)}) collective-permute-start(bf16[5,64,128]{2,1,0:T(8,128)(2,1)} %get-tuple-element.57), channel_id=1, source_target_pairs={{0,14},{1,15},{2,12},{3,13},{4,10},{5,11},{6,8},{7,9},{8,6},{9,7},... | collective-permute-start | bytes 245768 | tf_op jit(solution)/shard_map/ppermute | solution.py:282
  79.2 7.7 %collective-permute-start.6 = (bf16[5,64,128]{2,1,0:T(8,128)(2,1)S(1)}, bf16[5,64,128]{2,1,0:T(8,128)(2,1)}, u32[]{:S(2)}, u32[]{:S(2)}) collective-permute-start(bf16[5,64,128]{2,1,0:T(8,128)(2,1)S(1)} %get-tuple-element.56), channel_id=1, source_target_pairs={{0,4},{1,5},{2,6},{3,7},{4,0},{5,1},{6,2},{7,3},{8,12},{9,13},{10,... | collective-permute-start | bytes 245768 | tf_op jit(solution)/shard_map/ppermute | solution.py:282
  79.2 11.9 %collective-permute-start.7 = (bf16[5,64,128]{2,1,0:T(8,128)(2,1)S(1)}, bf16[5,64,128]{2,1,0:T(8,128)(2,1)}, u32[]{:S(2)}, u32[]{:S(2)}) collective-permute-start(bf16[5,64,128]{2,1,0:T(8,128)(2,1)S(1)} %get-tuple-element.62), channel_id=1, source_target_pairs={{0,8},{1,9},{2,10},{3,11},{4,12},{5,13},{6,14},{7,15},{8,0},{9,1},... | collective-permute-start | bytes 245768 | tf_op jit(solution)/shard_map/ppermute | solution.py:282
  83.3 7.7 %collective-permute-start.8 = (bf16[5,64,128]{2,1,0:T(8,128)(2,1)S(1)}, bf16[5,64,128]{2,1,0:T(8,128)(2,1)}, u32[]{:S(2)}, u32[]{:S(2)}) collective-permute-start(bf16[5,64,128]{2,1,0:T(8,128)(2,1)S(1)} %get-tuple-element.61), channel_id=1, source_target_pairs={{0,12},{1,13},{2,14},{3,15},{4,8},{5,9},{6,10},{7,11},{8,4},{9,5},... | collective-permute-start | bytes 245768 | tf_op jit(solution)/shard_map/ppermute | solution.py:282
  94.1 9.7 %collective-permute-start.14 = (bf16[5,64,128]{2,1,0:T(8,128)(2,1)S(1)}, bf16[5,64,128]{2,1,0:T(8,128)(2,1)S(1)}, u32[]{:S(2)}, u32[]{:S(2)}) collective-permute-start(bf16[5,64,128]{2,1,0:T(8,128)(2,1)S(1)} %get-tuple-element.38), channel_id=1, source_target_pairs={{0,8},{1,9},{2,10},{3,11},{4,12},{5,13},{6,14},{7,15},{8,0},{9,1},... | collective-permute-start | bytes 245768 | tf_op jit(solution)/shard_map/ppermute | solution.py:282
  95.1 11.6 %collective-permute-start.15 = (bf16[5,64,128]{2,1,0:T(8,128)(2,1)S(1)}, bf16[5,64,128]{2,1,0:T(8,128)(2,1)S(1)}, u32[]{:S(2)}, u32[]{:S(2)}) collective-permute-start(bf16[5,64,128]{2,1,0:T(8,128)(2,1)S(1)} %get-tuple-element.38), channel_id=1, source_target_pairs={{0,12},{1,13},{2,14},{3,15},{4,8},{5,9},{6,10},{7,11},{8,4},{9,5},... | collective-permute-start | bytes 245768 | tf_op jit(solution)/shard_map/ppermute | solution.py:282
  96.7 10.0 %collective-permute-start.16 = (bf16[5,64,128]{2,1,0:T(8,128)(2,1)S(1)}, bf16[5,64,128]{2,1,0:T(8,128)(2,1)S(1)}, u32[]{:S(2)}, u32[]{:S(2)}) collective-permute-start(bf16[5,64,128]{2,1,0:T(8,128)(2,1)S(1)} %get-tuple-element.38), channel_id=1, source_target_pairs={{0,2},{1,3},{2,0},{3,1},{4,6},{5,7},{6,4},{7,5},{8,10},{9,11},{10,... | collective-permute-start | bytes 245768 | tf_op jit(solution)/shard_map/ppermute | solution.py:282
  97.6 9.1 %collective-permute-start.17 = (bf16[5,64,128]{2,1,0:T(8,128)(2,1)S(1)}, bf16[5,64,128]{2,1,0:T(8,128)(2,1)S(1)}, u32[]{:S(2)}, u32[]{:S(2)}) collective-permute-start(bf16[5,64,128]{2,1,0:T(8,128)(2,1)S(1)} %get-tuple-element.38), channel_id=1, source_target_pairs={{0,6},{1,7},{2,4},{3,5},{4,2},{5,3},{6,0},{7,1},{8,14},{9,15},{10,... | collective-permute-start | bytes 245768 | tf_op jit(solution)/shard_map/ppermute | solution.py:282
  99.0 10.8 %collective-permute-start.18 = (bf16[5,64,128]{2,1,0:T(8,128)(2,1)S(1)}, bf16[5,64,128]{2,1,0:T(8,128)(2,1)S(1)}, u32[]{:S(2)}, u32[]{:S(2)}) collective-permute-start(bf16[5,64,128]{2,1,0:T(8,128)(2,1)S(1)} %get-tuple-element.38), channel_id=1, source_target_pairs={{0,10},{1,11},{2,8},{3,9},{4,14},{5,15},{6,12},{7,13},{8,2},{9,3},... | collective-permute-start | bytes 245768 | tf_op jit(solution)/shard_map/ppermute | solution.py:282
  132.5 9.6 %collective-permute-start.23 = (bf16[5,64,128]{2,1,0:T(8,128)(2,1)S(1)}, bf16[5,64,128]{2,1,0:T(8,128)(2,1)S(1)}, u32[]{:S(2)}, u32[]{:S(2)}) collective-permute-start(bf16[5,64,128]{2,1,0:T(8,128)(2,1)S(1)} %get-tuple-element.55), channel_id=1, source_target_pairs={{0,8},{1,9},{2,10},{3,11},{4,12},{5,13},{6,14},{7,15},{8,0},{9,1},... | collective-permute-start | bytes 245768 | tf_op jit(solution)/shard_map/ppermute | solution.py:282
  134.3 10.3 %collective-permute-start.24 = (bf16[5,64,128]{2,1,0:T(8,128)(2,1)S(1)}, bf16[5,64,128]{2,1,0:T(8,128)(2,1)S(1)}, u32[]{:S(2)}, u32[]{:S(2)}) collective-permute-start(bf16[5,64,128]{2,1,0:T(8,128)(2,1)S(1)} %get-tuple-element.54), channel_id=1, source_target_pairs={{0,12},{1,13},{2,14},{3,15},{4,8},{5,9},{6,10},{7,11},{8,4},{9,5},... | collective-permute-start | bytes 245768 | tf_op jit(solution)/shard_map/ppermute | solution.py:282
  135.7 8.9 %collective-permute-start.25 = (bf16[5,64,128]{2,1,0:T(8,128)(2,1)S(1)}, bf16[5,64,128]{2,1,0:T(8,128)(2,1)S(1)}, u32[]{:S(2)}, u32[]{:S(2)}) collective-permute-start(bf16[5,64,128]{2,1,0:T(8,128)(2,1)S(1)} %get-tuple-element.53), channel_id=1, source_target_pairs={{0,2},{1,3},{2,0},{3,1},{4,6},{5,7},{6,4},{7,5},{8,10},{9,11},{10,... | collective-permute-start | bytes 245768 | tf_op jit(solution)/shard_map/ppermute | solution.py:282
  136.7 7.9 %collective-permute-start.26 = (bf16[5,64,128]{2,1,0:T(8,128)(2,1)S(1)}, bf16[5,64,128]{2,1,0:T(8,128)(2,1)S(1)}, u32[]{:S(2)}, u32[]{:S(2)}) collective-permute-start(bf16[5,64,128]{2,1,0:T(8,128)(2,1)S(1)} %get-tuple-element.52), channel_id=1, source_target_pairs={{0,6},{1,7},{2,4},{3,5},{4,2},{5,3},{6,0},{7,1},{8,14},{9,15},{10,... | collective-permute-start | bytes 245768 | tf_op jit(solution)/shard_map/ppermute | solution.py:282
  137.5 11.0 %collective-permute-start.27 = (bf16[5,64,128]{2,1,0:T(8,128)(2,1)S(1)}, bf16[5,64,128]{2,1,0:T(8,128)(2,1)S(1)}, u32[]{:S(2)}, u32[]{:S(2)}) collective-permute-start(bf16[5,64,128]{2,1,0:T(8,128)(2,1)S(1)} %get-tuple-element.51), channel_id=1, source_target_pairs={{0,10},{1,11},{2,8},{3,9},{4,14},{5,15},{6,12},{7,13},{8,2},{9,3},... | collective-permute-start | bytes 245768 | tf_op jit(solution)/shard_map/ppermute | solution.py:282
  151.1 9.7 %collective-permute-start.30 = (bf16[5,64,128]{2,1,0:T(8,128)(2,1)S(1)}, bf16[5,64,128]{2,1,0:T(8,128)(2,1)S(1)}, u32[]{:S(2)}, u32[]{:S(2)}) collective-permute-start(bf16[5,64,128]{2,1,0:T(8,128)(2,1)S(1)} %get-tuple-element.34), channel_id=1, source_target_pairs={{0,8},{1,9},{2,10},{3,11},{4,12},{5,13},{6,14},{7,15},{8,0},{9,1},... | collective-permute-start | bytes 245768 | tf_op jit(solution)/shard_map/ppermute | solution.py:282
  152.4 11.1 %collective-permute-start.31 = (bf16[5,64,128]{2,1,0:T(8,128)(2,1)S(1)}, bf16[5,64,128]{2,1,0:T(8,128)(2,1)S(1)}, u32[]{:S(2)}, u32[]{:S(2)}) collective-permute-start(bf16[5,64,128]{2,1,0:T(8,128)(2,1)S(1)} %get-tuple-element.34), channel_id=1, source_target_pairs={{0,12},{1,13},{2,14},{3,15},{4,8},{5,9},{6,10},{7,11},{8,4},{9,5},... | collective-permute-start | bytes 245768 | tf_op jit(solution)/shard_map/ppermute | solution.py:282
  154.0 9.5 %collective-permute-start.32 = (bf16[5,64,128]{2,1,0:T(8,128)(2,1)S(1)}, bf16[5,64,128]{2,1,0:T(8,128)(2,1)S(1)}, u32[]{:S(2)}, u32[]{:S(2)}) collective-permute-start(bf16[5,64,128]{2,1,0:T(8,128)(2,1)S(1)} %get-tuple-element.34), channel_id=1, source_target_pairs={{0,2},{1,3},{2,0},{3,1},{4,6},{5,7},{6,4},{7,5},{8,10},{9,11},{10,... | collective-permute-start | bytes 245768 | tf_op jit(solution)/shard_map/ppermute | solution.py:282
  155.1 8.4 %collective-permute-start.33 = (bf16[5,64,128]{2,1,0:T(8,128)(2,1)S(1)}, bf16[5,64,128]{2,1,0:T(8,128)(2,1)S(1)}, u32[]{:S(2)}, u32[]{:S(2)}) collective-permute-start(bf16[5,64,128]{2,1,0:T(8,128)(2,1)S(1)} %get-tuple-element.34), channel_id=1, source_target_pairs={{0,6},{1,7},{2,4},{3,5},{4,2},{5,3},{6,0},{7,1},{8,14},{9,15},{10,... | collective-permute-start | bytes 245768 | tf_op jit(solution)/shard_map/ppermute | solution.py:282
  156.0 10.4 %collective-permute-start.34 = (bf16[5,64,128]{2,1,0:T(8,128)(2,1)S(1)}, bf16[5,64,128]{2,1,0:T(8,128)(2,1)S(1)}, u32[]{:S(2)}, u32[]{:S(2)}) collective-permute-start(bf16[5,64,128]{2,1,0:T(8,128)(2,1)S(1)} %get-tuple-element.34), channel_id=1, source_target_pairs={{0,10},{1,11},{2,8},{3,9},{4,14},{5,15},{6,12},{7,13},{8,2},{9,3},... | collective-permute-start | bytes 245768 | tf_op jit(solution)/shard_map/ppermute | solution.py:282
  185.7 7.7 %collective-permute-start.38 = (bf16[8,64,128]{2,1,0:T(8,128)(2,1)S(1)}, bf16[8,64,128]{2,1,0:T(8,128)(2,1)S(1)}, u32[]{:S(2)}, u32[]{:S(2)}) collective-permute-start(bf16[8,64,128]{2,1,0:T(8,128)(2,1)S(1)} %get-tuple-element.42), channel_id=1, source_target_pairs={{0,4},{1,5},{2,6},{3,7},{4,0},{5,1},{6,2},{7,3},{8,12},{9,13},{10,... | collective-permute-start | bytes 393224 | tf_op jit(solution)/shard_map/ppermute | solution.py:282
  186.4 12.9 %collective-permute-start.39 = (bf16[8,64,128]{2,1,0:T(8,128)(2,1)S(1)}, bf16[8,64,128]{2,1,0:T(8,128)(2,1)S(1)}, u32[]{:S(2)}, u32[]{:S(2)}) collective-permute-start(bf16[8,64,128]{2,1,0:T(8,128)(2,1)S(1)} %get-tuple-element.48), channel_id=1, source_target_pairs={{0,8},{1,9},{2,10},{3,11},{4,12},{5,13},{6,14},{7,15},{8,0},{9,1},... | collective-permute-start | bytes 393224 | tf_op jit(solution)/shard_map/ppermute | solution.py:282
  188.3 16.2 %collective-permute-start.40 = (bf16[8,64,128]{2,1,0:T(8,128)(2,1)}, bf16[8,64,128]{2,1,0:T(8,128)(2,1)S(1)}, u32[]{:S(2)}, u32[]{:S(2)}) collective-permute-start(bf16[8,64,128]{2,1,0:T(8,128)(2,1)} %get-tuple-element.47), channel_id=1, source_target_pairs={{0,12},{1,13},{2,14},{3,15},{4,8},{5,9},{6,10},{7,11},{8,4},{9,5},... | collective-permute-start | bytes 393224 | tf_op jit(solution)/shard_map/ppermute | solution.py:282
  190.1 14.4 %collective-permute-start.41 = (bf16[8,64,128]{2,1,0:T(8,128)(2,1)}, bf16[8,64,128]{2,1,0:T(8,128)(2,1)S(1)}, u32[]{:S(2)}, u32[]{:S(2)}) collective-permute-start(bf16[8,64,128]{2,1,0:T(8,128)(2,1)} %get-tuple-element.46), channel_id=1, source_target_pairs={{0,2},{1,3},{2,0},{3,1},{4,6},{5,7},{6,4},{7,5},{8,10},{9,11},{10,... | collective-permute-start | bytes 393224 | tf_op jit(solution)/shard_map/ppermute | solution.py:282
  191.1 13.4 %collective-permute-start.42 = (bf16[8,64,128]{2,1,0:T(8,128)(2,1)}, bf16[8,64,128]{2,1,0:T(8,128)(2,1)S(1)}, u32[]{:S(2)}, u32[]{:S(2)}) collective-permute-start(bf16[8,64,128]{2,1,0:T(8,128)(2,1)} %get-tuple-element.45), channel_id=1, source_target_pairs={{0,6},{1,7},{2,4},{3,5},{4,2},{5,3},{6,0},{7,1},{8,14},{9,15},{10,... | collective-permute-start | bytes 393224 | tf_op jit(solution)/shard_map/ppermute | solution.py:282
  193.4 16.9 %collective-permute-start.43 = (bf16[8,64,128]{2,1,0:T(8,128)(2,1)S(1)}, bf16[8,64,128]{2,1,0:T(8,128)(2,1)S(1)}, u32[]{:S(2)}, u32[]{:S(2)}) collective-permute-start(bf16[8,64,128]{2,1,0:T(8,128)(2,1)S(1)} %get-tuple-element.44), channel_id=1, source_target_pairs={{0,10},{1,11},{2,8},{3,9},{4,14},{5,15},{6,12},{7,13},{8,2},{9,3},... | collective-permute-start | bytes 393224 | tf_op jit(solution)/shard_map/ppermute | solution.py:282
  199.3 11.0 %collective-permute-start.44 = (bf16[8,64,128]{2,1,0:T(8,128)(2,1)S(1)}, bf16[8,64,128]{2,1,0:T(8,128)(2,1)S(1)}, u32[]{:S(2)}, u32[]{:S(2)}) collective-permute-start(bf16[8,64,128]{2,1,0:T(8,128)(2,1)S(1)} %get-tuple-element.43), channel_id=1, source_target_pairs={{0,14},{1,15},{2,12},{3,13},{4,10},{5,11},{6,8},{7,9},{8,6},{9,7},... | collective-permute-start | bytes 393224 | tf_op jit(solution)/shard_map/ppermute | solution.py:282
  (28 other events, 271.8 us)
